TPU v7x, 256 devices: a whole 4x4x8 slice. The times are simulated.
256 devices in a mesh: ep: 16 (over z, core), sp: 16 (over x, y).
Axes of the slice: x: 4, y: 4, z: 8, core: 2. Of those that a mesh axis runs over, the one named last changes fastest.
Arguments:
- queries: bfloat16 [65536, 2048], P(('ep', 'sp')), may hold values from -6 to 6
- keys: bfloat16 [65536, 2048], P(('ep', 'sp')), may hold values from -6 to 6
- values: bfloat16 [65536, 2048], P(('ep', 'sp')), may hold values from -6 to 6
- residual: bfloat16 [65536, 2048], P('ep', 'sp'), may hold values from -6 to 6
- cotangent: bfloat16 [65536, 2048], P('ep', 'sp'), may hold values from -1.5 to 1.5
- gate_proj: bfloat16 [16, 2048, 4096], P('ep', None, 'sp'), may hold values from -0.1875 to 0.1875
- up_proj: bfloat16 [16, 2048, 4096], P('ep', None, 'sp'), may hold values from -0.125 to 0.125
- down_proj: bfloat16 [16, 4096, 2048], P('ep', 'sp'), may hold values from -0.125 to 0.125
- chosen: int32 [16, 16, 32], P('ep'), may hold values from 0 to 4095, as said below
- counts: int32 [16, 16], P('ep'), may hold values from 0 to 32, as said below
- route_weight: float32 [16, 16, 32], P('ep'), may hold values from 0.5 to 3
Outputs:
- block_out: bfloat16 [65536, 2048], P('ep', 'sp')
- grad_hidden: bfloat16 [65536, 2048], P('ep', 'sp')
- grad_down: bfloat16 [16, 4096, 2048], P('ep', 'sp')
Inputs may be any that keep to these rules, and one draw needn't show every extreme that they name: `chosen`: the 32 positions of one list (one image, one expert) are distinct. The live slots of a list are its first counts[a, e]; in every draw some expert has all 32 slots live in every image.
All inputs are finite; a program needn't handle non-finite values.
Results may differ from a plain program's by a relative error of at most 0.014.
Values may be sent and summed in bfloat16 or wider, within the bound.
No kernel may reach another device: no remote copies, remote signals or barrier semaphores. Data moves between devices by JAX's collectives and lax.ppermute only.
A program may use at most 64 MiB of HBM per device.

v0:
```python
import functools
import math

import jax
import jax.numpy as jnp
from jax import lax
from jax.sharding import PartitionSpec as P

HD = 128
SLOTS = 32


def score_block(query_block, key_heads, value_heads):
    scores = jnp.einsum(
        "qhd,khd->hqk", query_block, key_heads, preferred_element_type=jnp.float32
    ) * HD ** (-0.5)
    top = jnp.max(scores, axis=-1, keepdims=True)
    expd = jnp.exp(scores - top)
    probs = (expd / jnp.sum(expd, axis=-1, keepdims=True)).astype(jnp.bfloat16)
    return jnp.einsum(
        "hqk,khd->qhd", probs, value_heads, preferred_element_type=jnp.float32
    ).astype(jnp.bfloat16)


def attend(query_all, key_all, value_all):
    length = query_all.shape[0]
    heads_here = query_all.shape[1] // HD
    block_rows = math.gcd(length, 512)
    query_blocks = query_all.reshape(length // block_rows, block_rows, heads_here, HD)
    key_heads = key_all.reshape(length, heads_here, HD)
    value_heads = value_all.reshape(length, heads_here, HD)
    result = lax.map(
        functools.partial(score_block, key_heads=key_heads, value_heads=value_heads), query_blocks
    )
    return result.reshape(length, heads_here * HD)


def to_owners(buffer):
    return lax.all_to_all(buffer, "ep", split_axis=1, concat_axis=1, tiled=True)


def to_group(buffer):
    return lax.all_gather(buffer, "sp", axis=3, tiled=True)


def group_sum(term_fn):
    return lax.psum_scatter(
        term_fn(jnp.int32(0), 1 * lax.axis_size("sp")).astype(jnp.bfloat16),
        "sp",
        scatter_dimension=0,
        tiled=True,
    ).astype(jnp.float32)


def to_sources(buffer):
    return lax.all_to_all(buffer, "ep", split_axis=1, concat_axis=1, tiled=True)


def expert_forward(rows, gate_here, up_here):
    gate_pre = jnp.dot(rows, gate_here, preferred_element_type=jnp.float32)
    up_pre = jnp.dot(rows, up_here, preferred_element_type=jnp.float32)
    activation = (jax.nn.silu(gate_pre) * up_pre).astype(jnp.bfloat16)
    return (gate_pre, up_pre, activation)


def expert_backward(tangent, gate_pre, up_pre, activation, down_here):
    grad_local = lax.dot_general(
        activation, tangent, (((0,), (0,)), ((), ())), preferred_element_type=jnp.float32
    )
    d_act = lax.dot_general(
        tangent, down_here, (((1,), (1,)), ((), ())), preferred_element_type=jnp.float32
    )
    sig_gate = jax.nn.sigmoid(gate_pre)
    d_gate = (d_act * up_pre * sig_gate * (1.0 + gate_pre * (1.0 - sig_gate))).astype(jnp.bfloat16)
    d_up = (d_act * jax.nn.silu(gate_pre)).astype(jnp.bfloat16)
    return (grad_local.astype(jnp.bfloat16), d_gate, d_up)


def down_terms(activation, down_here, col_width):

    def partial_out(first_block, blocks):
        columns = down_here
        columns = columns.reshape(columns.shape[0], blocks, col_width)
        return jnp.einsum("rf,fcd->crd", activation, columns, preferred_element_type=jnp.float32)[
            :, None
        ]

    return partial_out


def back_terms(d_gate, d_up, gate_here, up_here, col_width):

    def partial_grad(first_block, blocks):
        gate_rows = gate_here
        up_rows = up_here
        gate_rows = gate_rows.reshape(blocks, col_width, gate_rows.shape[1])
        up_rows = up_rows.reshape(blocks, col_width, up_rows.shape[1])
        summed = jnp.einsum("rf,cdf->crd", d_gate, gate_rows, preferred_element_type=jnp.float32)
        summed = summed + jnp.einsum(
            "rf,cdf->crd", d_up, up_rows, preferred_element_type=jnp.float32
        )
        return summed[:, None]

    return partial_grad


def on_device(
    queries,
    keys,
    values,
    residual,
    cotangent,
    gate_proj,
    up_proj,
    down_proj,
    chosen,
    counts,
    route_weight,
):
    head_major = (
        lax.all_to_all(queries, "sp", split_axis=1, concat_axis=0, tiled=True),
        lax.all_to_all(keys, "sp", split_axis=1, concat_axis=0, tiled=True),
        lax.all_to_all(values, "sp", split_axis=1, concat_axis=0, tiled=True),
    )
    attended = attend(head_major[0], head_major[1], head_major[2])
    hidden = (residual.astype(jnp.float32) + attended.astype(jnp.float32)).astype(jnp.bfloat16)
    length = hidden.shape[0]
    col_width = hidden.shape[1]
    places = chosen[0]
    expert_count = places.shape[0]
    live_slot = jnp.arange(SLOTS, dtype=jnp.int32)[None, :] < counts[0][:, None]
    weight = jnp.where(live_slot, route_weight[0], jnp.float32(0.0))
    flat_places = places.reshape(-1)
    rows_x = jnp.take(hidden, flat_places, axis=0).reshape(expert_count, SLOTS, col_width)
    rows_dy = jnp.take(cotangent, flat_places, axis=0).reshape(expert_count, SLOTS, col_width)
    rows_dy = (rows_dy.astype(jnp.float32) * weight[..., None]).astype(jnp.bfloat16)
    gate_here = gate_proj[0]
    up_here = up_proj[0]
    down_here = down_proj[0]
    owned_rows = to_group(to_owners(rows_x[None]))
    sources = owned_rows.shape[1]
    row_total = sources * SLOTS
    gathered_x = owned_rows[0].reshape(row_total, -1)
    gate_pre, up_pre, activation = expert_forward(gathered_x, gate_here, up_here)
    summed = group_sum(down_terms(activation, down_here, col_width))
    expert_out = to_sources(summed.reshape(1, sources, SLOTS, col_width).astype(jnp.bfloat16))[0]
    owned_grads = to_group(to_owners(rows_dy[None]))
    tangent = owned_grads[0].reshape(row_total, -1)
    grad_local, d_gate, d_up = expert_backward(tangent, gate_pre, up_pre, activation, down_here)
    summed_grads = group_sum(back_terms(d_gate, d_up, gate_here, up_here, col_width))
    d_rows = to_sources(summed_grads.reshape(1, sources, SLOTS, col_width).astype(jnp.bfloat16))[0]
    flat_weight = weight.reshape(-1)
    combined = (
        jnp.zeros((length, col_width), jnp.float32)
        .at[flat_places]
        .add(expert_out.reshape(-1, col_width).astype(jnp.float32) * flat_weight[:, None])
    )
    block_out = (hidden.astype(jnp.float32) + combined).astype(jnp.bfloat16)
    row_grads = (
        jnp.zeros((length, col_width), jnp.float32)
        .at[flat_places]
        .add(d_rows.reshape(-1, col_width).astype(jnp.float32))
    )
    grad_hidden = (cotangent.astype(jnp.float32) + row_grads).astype(jnp.bfloat16)
    return (block_out, grad_hidden, grad_local[None])


def solution(mesh):
    in_specs = (
        P(("ep", "sp"), None),
        P(("ep", "sp"), None),
        P(("ep", "sp"), None),
        P("ep", "sp"),
        P("ep", "sp"),
        P("ep", None, "sp"),
        P("ep", None, "sp"),
        P("ep", "sp", None),
        P("ep", None, None),
        P("ep", None),
        P("ep", None, None),
    )
    out_specs = (P("ep", "sp"), P("ep", "sp"), P("ep", "sp", None))
    return jax.shard_map(
        on_device, mesh=mesh, in_specs=in_specs, out_specs=out_specs, check_vma=False
    )
```

profile of v0, /device:TPU:1, one launch (start us, length us, event | category | flops | bytes accessed | tf_op | source)
XLA Modules:
  0.0 443.9 jit_solution(12822008521743507940)
XLA Ops:
  7.2 2.4 copy.28
  9.6 7.6 %all-to-all-start = ((bf16[256,16,128]{0,2,1:T(8,128)(2,1)}), bf16[256,16,128]{0,2,1:T(8,128)(2,1)S(1)}, u32[]{:S(2)}, u32[]{:S(2)}) async-start(bf16[256,16,128]{0,2,1:T(8,128)(2,1)} %bitcast.7), calls=%async_computation | async-start | bytes 2097152 | tf_op jit(solution)/shard_map/all_to_all | solution.py:121
  18.5 14.2 %all-to-all-done = bf16[256,16,128]{0,2,1:T(8,128)(2,1)S(1)} async-done(((bf16[256,16,128]{0,2,1:T(8,128)(2,1)}), bf16[256,16,128]{0,2,1:T(8,128)(2,1)S(1)}, u32[]{:S(2)}, u32[]{:S(2)}) %all-to-all-start) | async-done | bytes 1048608 | tf_op jit(solution)/shard_map/all_to_all | solution.py:121
  32.7 4.3 all-to-all-start.1
  37.1 2.4 copy.32
  39.4 11.8 %all-to-all-done.1 = bf16[256,16,128]{0,2,1:T(8,128)(2,1)} async-done(((bf16[256,16,128]{0,2,1:T(8,128)(2,1)}), bf16[256,16,128]{0,2,1:T(8,128)(2,1)}, u32[]{:S(2)}, u32[]{:S(2)}) %all-to-all-start.1) | async-done | bytes 1048608 | tf_op jit(solution)/shard_map/all_to_all | solution.py:122
  51.3 4.8 %all-to-all-start.2 = ((bf16[256,16,128]{0,2,1:T(8,128)(2,1)}), bf16[256,16,128]{0,2,1:T(8,128)(2,1)}, u32[]{:S(2)}, u32[]{:S(2)}) async-start(bf16[256,16,128]{0,2,1:T(8,128)(2,1)} %bitcast.128), calls=%async_computation.2 | async-start | bytes 2097152 | tf_op jit(solution)/shard_map/all_to_all | solution.py:123
  56.3 1.3 gather_fusion.1
  58.3 1.6 copy.31
  59.9 7.9 %all-to-all-done.2 = bf16[256,16,128]{0,2,1:T(8,128)(2,1)} async-done(((bf16[256,16,128]{0,2,1:T(8,128)(2,1)}), bf16[256,16,128]{0,2,1:T(8,128)(2,1)}, u32[]{:S(2)}, u32[]{:S(2)}) %all-to-all-start.2) | async-done | bytes 1048608 | tf_op jit(solution)/shard_map/all_to_all | solution.py:123
  67.8 2.3 copy.33
  70.1 47.8 %while.10 = (s32[]{:T(128)}, bf16[8,512,1,128]{3,1,2,0:T(8,128)(2,1)}, bf16[8,512,1,128]{3,1,2,0:T(8,128)(2,1)S(1)}, bf16[4096,1,128]{2,0,1:T(8,128)(2,1)S(1)}, bf16[4096,1,128]{2,0,1:T(8,128)(2,1)}, /*index=5*/s32[]{:T(128)}) while((s32[]{:T(128)}, bf16[8,512,1,128]{3,1,2,0:T(8,128)(2,1)}, bf16[8,512,1,128]{3,1,2,0:T(8,128)(2,1)S(1)}, ...), condition=%wide.region_3.4_spmd, body=%wide.region_0.3_spmd.sunk | while | flops 1092680704 | bytes 31729776 | solution.py:32
  71.4 1.5 fusion.49
  73.0 3.1 fusion.50
  77.4 1.5 fusion.49
  78.9 3.1 fusion.50
  83.4 1.5 fusion.49
  84.9 3.1 fusion.50
  89.4 1.5 fusion.49
  90.9 3.1 fusion.50
  95.4 1.5 fusion.49
  96.9 3.1 fusion.50
  101.3 1.5 fusion.49
  102.8 3.1 fusion.50
  107.3 1.5 fusion.49
  108.8 3.1 fusion.50
  113.3 1.5 fusion.49
  114.8 3.1 fusion.50
  117.9 3.1 fusion.36
  122.6 24.1 %all_to_all.68 = bf16[1,16,32,128]{3,2,0,1:T(8,128)(2,1)} all-to-all(bf16[1,16,32,128]{3,2,0,1:T(8,128)(2,1)S(1)} %bitcast.138), channel_id=1, replica_groups=mesh['ep'=16,'sp'=16] {'ep'}, dimensions={1} | all-to-all | bytes 262144 | tf_op jit(solution)/shard_map/all_to_all | solution.py:39
  147.0 11.7 %all_to_all.69 = bf16[1,16,32,128]{3,2,0,1:T(8,128)(2,1)} all-to-all(bf16[1,16,32,128]{3,2,0,1:T(8,128)(2,1)S(1)} %fusion.27), channel_id=1, replica_groups=mesh['ep'=16,'sp'=16] {'ep'}, dimensions={1} | all-to-all | bytes 262144 | tf_op jit(solution)/shard_map/all_to_all | solution.py:39
  158.7 1.5 copy.44
  160.2 31.4 %all-gather.3.cloned.1.call-done = bf16[1,16,32,2048]{3,2,0,1:T(8,128)(2,1)} async-done(((bf16[1,16,32,128]{3,2,0,1:T(8,128)(2,1)}), bf16[1,16,32,2048]{3,2,0,1:T(8,128)(2,1)}) %all-gather.3.cloned.1.call-update) | async-done | bytes 2097168 | tf_op jit(solution)/shard_map/all_gather | solution.py:43
  191.6 2.4 fusion.19
  194.1 1.5 multiply_convert_fusion.2
  195.6 2.1 convert_bitcast_fusion
  197.9 48.2 %all-gather.5.cloned.1.call-done = bf16[1,16,32,2048]{3,2,0,1:T(8,128)(2,1)} async-done(((bf16[1,16,32,128]{3,2,0,1:T(8,128)(2,1)}), bf16[1,16,32,2048]{3,2,0,1:T(8,128)(2,1)}) %all-gather.5.cloned.1.call-update) | async-done | bytes 2097168 | tf_op jit(solution)/shard_map/all_gather | solution.py:43
  246.1 2.4 fusion.15
  249.5 2.1 fusion.14
  252.3 75.4 %reduce-scatter.13.cloned.1.call-done = bf16[1,1,512,128]{3,2,0,1:T(8,128)(2,1)} async-done(((bf16[16,1,512,128]{3,2,0,1:T(8,128)(2,1)}), bf16[1,1,512,128]{3,2,0,1:T(8,128)(2,1)}) %reduce-scatter.13.cloned.1.call-update) | async-done | bytes 131088
  327.7 9.3 %all-to-all-start.4 = ((bf16[1,16,32,128]{3,2,0,1:T(8,128)(2,1)}), bf16[1,16,32,128]{3,2,0,1:T(8,128)(2,1)S(1)}, u32[]{:S(2)}, u32[]{:S(2)}) async-start(bf16[1,16,32,128]{3,2,0,1:T(8,128)(2,1)} %bitcast.139), calls=%async_computation.4 | async-start | bytes 262144 | tf_op jit(solution)/shard_map/all_to_all | solution.py:56
  337.2 1.4 convert_element_type.144
  338.7 71.6 %reduce-scatter.15.cloned.1.call-done = bf16[1,1,512,128]{3,2,0,1:T(8,128)(2,1)} async-done(((bf16[16,1,512,128]{3,2,0,1:T(8,128)(2,1)}), bf16[1,1,512,128]{3,2,0,1:T(8,128)(2,1)}) %reduce-scatter.15.cloned.1.call-update) | async-done | bytes 131088
  410.4 9.4 %all-to-all-start.6 = ((bf16[1,16,32,128]{3,2,0,1:T(8,128)(2,1)}), bf16[1,16,32,128]{3,2,0,1:T(8,128)(2,1)}, u32[]{:S(2)}, u32[]{:S(2)}) async-start(bf16[1,16,32,128]{3,2,0,1:T(8,128)(2,1)} %bitcast.140), calls=%async_computation.6 | async-start | bytes 262144 | tf_op jit(solution)/shard_map/all_to_all | solution.py:56
  419.7 3.3 fusion.12
  423.0 6.2 %scatter_custom_fusion = f32[4096,128]{1,0:T(8,128)} fusion(f32[4096,128]{1,0:T(8,128)} %get-tuple-element.57, s32[512]{0:T(512)} %bitcast.143, bf16[512,128]{1,0:T(8,128)(2,1)S(1)} %bitcast.136, f32[512]{0:T(512)S(1)} %broadcast_select_fusion.2), kind=kCustom, calls=%fused_computation.44 | custom fusion | flops 196608 | bytes 2230272 | tf_op jit(solution)/shard_map/scatter-add | solution.py:156
  429.2 2.7 convert_element_type.143
  431.8 4.4 scatter_custom_fusion.1
  (77 shorter events, 17.7 us)
Async XLA Ops:
  7.2 186.9 %copy-start = (bf16[1,2048,256]{2,1,0:T(8,128)(2,1)S(1)}, bf16[1,2048,256]{2,1,0:T(8,128)(2,1)}, u32[]{:S(2)}) copy-start(bf16[1,2048,256]{2,1,0:T(8,128)(2,1)} %param.21) | copy-start | bytes 3145732
  7.2 10.0 %copy-start.5 = (bf16[256,2048]{1,0:T(8,128)(2,1)S(1)}, bf16[256,2048]{1,0:T(8,128)(2,1)}, u32[]{:S(2)}) copy-start(bf16[256,2048]{1,0:T(8,128)(2,1)} %param.16) | copy-start | bytes 3145732
  9.6 23.1 %all-to-all-start = ((bf16[256,16,128]{0,2,1:T(8,128)(2,1)}), bf16[256,16,128]{0,2,1:T(8,128)(2,1)S(1)}, u32[]{:S(2)}, u32[]{:S(2)}) async-start(bf16[256,16,128]{0,2,1:T(8,128)(2,1)} %bitcast.7), calls=%async_computation | async-start | bytes 2097152 | tf_op jit(solution)/shard_map/all_to_all | solution.py:121
  32.7 18.6 %all-to-all-start.1 = ((bf16[256,16,128]{0,2,1:T(8,128)(2,1)}), bf16[256,16,128]{0,2,1:T(8,128)(2,1)}, u32[]{:S(2)}, u32[]{:S(2)}) async-start(bf16[256,16,128]{0,2,1:T(8,128)(2,1)} %bitcast.11), calls=%async_computation.1 | async-start | bytes 2097152 | tf_op jit(solution)/shard_map/all_to_all | solution.py:122
  37.1 19.1 %copy-start.9 = (s32[1,16,32]{2,1,0:T(8,128)S(1)}, s32[1,16,32]{2,1,0:T(8,128)}, u32[]{:S(2)}) copy-start(s32[1,16,32]{2,1,0:T(8,128)} %param.23) | copy-start | bytes 6148
  37.1 19.2 %copy-start.1 = (bf16[4096,128]{1,0:T(8,128)(2,1)S(1)}, bf16[4096,128]{1,0:T(8,128)(2,1)}, u32[]{:S(2)}) copy-start(bf16[4096,128]{1,0:T(8,128)(2,1)} %param.19) | copy-start | bytes 3145732
  51.3 16.6 %all-to-all-start.2 = ((bf16[256,16,128]{0,2,1:T(8,128)(2,1)}), bf16[256,16,128]{0,2,1:T(8,128)(2,1)}, u32[]{:S(2)}, u32[]{:S(2)}) async-start(bf16[256,16,128]{0,2,1:T(8,128)(2,1)} %bitcast.128), calls=%async_computation.2 | async-start | bytes 2097152 | tf_op jit(solution)/shard_map/all_to_all | solution.py:123
  56.1 135.5 %all-gather.3.cloned.1.call-start = ((), (), s32[]{:S(2)}) async-start(), calls=%async_computation.9 | async-start | bytes 2228224 | tf_op jit(solution)/shard_map/all_gather | solution.py:43
  71.4 1.5 copy-start.7
  77.4 1.5 copy-start.7
  83.4 1.5 copy-start.7
  89.4 1.5 copy-start.7
  95.3 1.5 copy-start.7
  101.3 1.5 copy-start.7
  107.3 1.5 copy-start.7
  113.3 1.5 copy-start.7
  121.1 25.6 %copy-start.10 = (f32[1,16,32]{2,1,0:T(8,128)S(1)}, f32[1,16,32]{2,1,0:T(8,128)}, u32[]{:S(2)}) copy-start(f32[1,16,32]{2,1,0:T(8,128)} %param.25) | copy-start | bytes 6148
  121.1 25.7 %copy-start.11 = (s32[1,16]{1,0:T(1,128)S(1)}, s32[1,16]{1,0:T(1,128)}, u32[]{:S(2)}) copy-start(s32[1,16]{1,0:T(1,128)} %param.24) | copy-start | bytes 196
  122.4 69.2 %copy-start.2 = (bf16[1,2048,256]{2,1,0:T(8,128)(2,1)S(1)}, bf16[1,2048,256]{2,1,0:T(8,128)(2,1)}, u32[]{:S(2)}) copy-start(bf16[1,2048,256]{2,1,0:T(8,128)(2,1)} %param.20) | copy-start | bytes 3145732
  146.7 99.5 %all-gather.5.cloned.1.call-start = ((), (), s32[]{:S(2)}) async-start(), calls=%async_computation.10 | async-start | bytes 2228224 | tf_op jit(solution)/shard_map/all_gather | solution.py:43
  158.7 169.1 %reduce-scatter.13.cloned.1.call-start = ((), (), s32[]{:S(2)}) async-start(), calls=%async_computation.11 | async-start | bytes 2228224
  191.6 2.5 copy-start.12
  194.1 1.5 copy-start.3
  197.7 48.5 %copy-start.6 = (bf16[1,256,2048]{2,1,0:T(8,128)(2,1)S(1)}, bf16[1,256,2048]{2,1,0:T(8,128)(2,1)}, u32[]{:S(2)}) copy-start(bf16[1,256,2048]{2,1,0:T(8,128)(2,1)} %param.22) | copy-start | bytes 3145732
  197.7 212.7 %reduce-scatter.15.cloned.1.call-start = ((), (), s32[]{:S(2)}) async-start(), calls=%async_computation.12 | async-start | bytes 2228224
  246.1 2.4 copy-start.4
  246.1 2.4 copy-start.8
  327.7 82.6 %all-to-all-start.4 = ((bf16[1,16,32,128]{3,2,0,1:T(8,128)(2,1)}), bf16[1,16,32,128]{3,2,0,1:T(8,128)(2,1)S(1)}, u32[]{:S(2)}, u32[]{:S(2)}) async-start(bf16[1,16,32,128]{3,2,0,1:T(8,128)(2,1)} %bitcast.139), calls=%async_computation.4 | async-start | bytes 262144 | tf_op jit(solution)/shard_map/all_to_all | solution.py:56
  410.4 21.5 %all-to-all-start.6 = ((bf16[1,16,32,128]{3,2,0,1:T(8,128)(2,1)}), bf16[1,16,32,128]{3,2,0,1:T(8,128)(2,1)}, u32[]{:S(2)}, u32[]{:S(2)}) async-start(bf16[1,16,32,128]{3,2,0,1:T(8,128)(2,1)} %bitcast.140), calls=%async_computation.6 | async-start | bytes 262144 | tf_op jit(solution)/shard_map/all_to_all | solution.py:56
Sparse Core Ops, SparseCore 0:
  146.8 44.7 all-gather.2
  194.0 52.0 all-gather.4
  249.7 78.0 reduce-scatter.12
  331.6 78.7 reduce-scatter.14
where the time goes:
time: 445 us; the launch traced here: 444 us
  waiting for transfers between devices  261 us (59%)
  matrix products  50.4 us (11%)
  starting transfers between devices  35.8 us (8%)
  blocking collectives  35.8 us (8%)
  other arithmetic  31.9 us (7%)
  local copies, waits for them, and re-layouts  15.1 us (3%)
  between operations  14 us (3%)
    unnamed x6, waiting for transfers between devices  147 us
    all_gather x2, waiting for transfers between devices, to_group(): return lax.all_gather(buffer, 'sp', axis=3, tiled=True)  79.6 us
    all_to_all x2, blocking collectives, to_owners(): return lax.all_to_all(buffer, 'ep', split_axis=1, concat_axis=1, tiled=True)  35.8 us
    dot_general x8, matrix products, score_block(): jnp.einsum('hqk,khd->qhd', probs, value_heads, preferred_element_type=jnp...  25.1 us
    all_to_all x2, starting transfers between devices, to_sources(): return lax.all_to_all(buffer, 'ep', split_axis=1, concat_axis=1, tiled=True)  18.7 us
    all_to_all x1, waiting for transfers between devices, on_device(): lax.all_to_all(queries, 'sp', split_axis=1, concat_axis=0, tiled=True)  14.2 us
    reduce_sum x8, other arithmetic, score_block(): probs = (expd / jnp.sum(expd, axis=-1, keepdims=True)).astype(jnp.bfloat16)  12 us
    all_to_all x1, waiting for transfers between devices, on_device(): lax.all_to_all(keys, 'sp', split_axis=1, concat_axis=0, tiled=True)  11.8 us
  transfers between devices with their start and end apart: 9, of which 7 were waited for; matrix products, arithmetic and copies ran while one was open for 8% of the time, Pallas kernels for 0%

commit v1 on v0

v1 whole, which is shorter than its diff:
```python
import functools

import jax
import jax.numpy as jnp
from jax import lax
from jax.experimental import pallas as pl
from jax.experimental.pallas import tpu as pltpu
from jax.sharding import PartitionSpec as P

HD = 128
SLOTS = 32
SIDE = 4
LOG2E = 1.4426950408889634
VMEM_LIMIT = 48 * 1024 * 1024
BIG_VMEM = 60 * 1024 * 1024
SAFE_EXPONENT = 110.0
F32 = jnp.float32
BF16 = jnp.bfloat16
OVER_LAST = (((1,), (1,)), ((), ()))


def params(limit=VMEM_LIMIT):
    return pltpu.CompilerParams(vmem_limit_bytes=limit)


def pack_kernel(q_ref, k_ref, v_ref, out_ref):
    rows, width = q_ref.shape
    for h in range(width // HD):
        here = slice(h * HD, (h + 1) * HD)
        out_ref[h, 0:rows, :] = q_ref[:, here]
        out_ref[h, rows : 2 * rows, :] = k_ref[:, here]
        out_ref[h, 2 * rows : 3 * rows, :] = v_ref[:, here]


def pack(queries, keys, values):
    rows, width = queries.shape
    heads = width // HD
    steps = 4
    columns = pl.BlockSpec((rows, width // steps), lambda h: (0, h))
    return pl.pallas_call(
        pack_kernel,
        grid=(steps,),
        in_specs=[columns] * 3,
        out_specs=pl.BlockSpec((heads // steps, 3 * rows, HD), lambda h: (h, 0, 0)),
        out_shape=jax.ShapeDtypeStruct((heads, 3 * rows, HD), BF16),
        compiler_params=params(BIG_VMEM),
        name="pack_qkv",
    )(queries, keys, values)


def attention_kernel(rows, q_ref, res_ref, qkv_ref, out_ref, peak_ref):
    sources = qkv_ref.shape[0]
    block = res_ref.shape[0]
    part = min(256, block)
    scale = HD**-0.5 * LOG2E

    @pl.when(pl.program_id(0) == 0)
    def _():
        peak = jnp.zeros((rows, HD), F32)
        for s in range(sources):
            key = qkv_ref[s, rows : 2 * rows, :].astype(F32)
            square = (key * key).astype(BF16)
            peak = jnp.maximum(
                peak, jnp.dot(square, jnp.ones((HD, HD), BF16), preferred_element_type=F32)
            )
        peak_ref[0] = jnp.max(peak)

    query = q_ref[...].reshape(block, HD)
    wide_query = query.astype(F32)
    longest = jnp.max(jnp.sum(wide_query * wide_query, axis=1, keepdims=True))
    small = longest * peak_ref[0] * (1.02 * scale * scale) <= SAFE_EXPONENT * SAFE_EXPONENT

    def scores_of(here, s):
        return (
            lax.dot_general(
                query[here], qkv_ref[s, rows : 2 * rows, :], OVER_LAST, preferred_element_type=F32
            )
            * scale
        )

    def finish(here, total, norm):
        norm = jnp.sum(norm, axis=1, keepdims=True)
        attended = (total / norm).astype(BF16)
        out_ref[here, :] = (res_ref[here, :].astype(F32) + attended.astype(F32)).astype(BF16)

    def add_up(here, shift):
        total = jnp.zeros((part, HD), F32)
        norm = jnp.zeros((part, HD), F32)
        for s in range(sources):
            scores = scores_of(here, s)
            probs = jnp.exp2(scores if shift is None else scores - shift)
            for c in range(rows // HD):
                norm = norm + probs[:, c * HD : (c + 1) * HD]
            total = total + jnp.dot(
                probs.astype(BF16), qkv_ref[s, 2 * rows : 3 * rows, :], preferred_element_type=F32
            )
        finish(here, total, norm)

    @pl.when(small)
    def _():
        for p in range(block // part):
            add_up(slice(p * part, (p + 1) * part), None)

    @pl.when(jnp.logical_not(small))
    def _():
        for p in range(block // part):
            here = slice(p * part, (p + 1) * part)
            top = jnp.full((part, 1), -jnp.inf, F32)
            for s in range(sources):
                top = jnp.maximum(top, jnp.max(scores_of(here, s), axis=1, keepdims=True))
            add_up(here, top)


def attention(queries, query_spec, residual, residual_first, total, qkv, block, name):
    sources, rows3, _ = qkv.shape
    rows = rows3 // 3
    length = sources * rows
    return pl.pallas_call(
        functools.partial(attention_kernel, rows),
        grid=(total // block,),
        in_specs=[
            query_spec,
            pl.BlockSpec((block, HD), lambda i: (i + residual_first, 0)),
            pl.BlockSpec((sources, rows3, HD), lambda i: (0, 0, 0)),
        ],
        out_specs=pl.BlockSpec((block, HD), lambda i: (i, 0)),
        out_shape=jax.ShapeDtypeStruct((total, HD), BF16),
        scratch_shapes=[pltpu.SMEM((1,), F32)],
        compiler_params=params(),
        cost_estimate=pl.CostEstimate(
            flops=8 * total * length * HD,
            bytes_accessed=4 * total * HD * 2 + qkv.size * 2,
            transcendentals=total * length,
        ),
        name=name,
    )(queries, residual, qkv)


def wide_rows(ref):
    return jnp.concatenate([ref[c] for c in range(ref.shape[0])], axis=1)


def tangent_kernel(tan_ref, down_ref, d_act_ref):
    d_act_ref[...] = lax.dot_general(
        wide_rows(tan_ref), down_ref[...], OVER_LAST, preferred_element_type=F32
    )


def tangent_product(tangent, down):
    blocks, total, width = tangent.shape
    hidden = down.shape[0]
    return pl.pallas_call(
        tangent_kernel,
        out_shape=jax.ShapeDtypeStruct((total, hidden), F32),
        compiler_params=params(),
        cost_estimate=pl.CostEstimate(
            flops=2 * total * hidden * blocks * width,
            bytes_accessed=2 * tangent.size + 2 * down.size + 4 * total * hidden,
            transcendentals=0,
        ),
        name="tangent_product",
    )(tangent, down)


def expert_kernel(
    me_ref, x_ref, d_act_ref, gate_ref, up_ref, down_ref, act_ref, out_ref, *grad_refs
):
    rows = wide_rows(x_ref)
    gate_pre = jnp.dot(rows, gate_ref[...], preferred_element_type=F32)
    up_pre = jnp.dot(rows, up_ref[...], preferred_element_type=F32)
    sig = jax.nn.sigmoid(gate_pre)
    silu = gate_pre * sig
    act = (silu * up_pre).astype(BF16)
    act_ref[...] = act
    d_act = d_act_ref[...]
    d_gate = (d_act * up_pre * sig * (1.0 + gate_pre * (1.0 - sig))).astype(BF16)
    d_up = (d_act * silu).astype(BF16)
    blocks, _, width = out_ref.shape
    side = len(grad_refs)
    for d in range(side):
        y = lax.rem(me_ref[0] + d, side)
        for x in range(0, side, 2):
            first = pl.ds(pl.multiple_of((x * side + y) * width, width), width)
            second = pl.ds(pl.multiple_of(((x + 1) * side + y) * width, width), width)
            gate = jnp.concatenate([gate_ref[first, :], gate_ref[second, :]], axis=0)
            up = jnp.concatenate([up_ref[first, :], up_ref[second, :]], axis=0)
            pair = lax.dot_general(d_gate, gate, OVER_LAST, preferred_element_type=F32)
            pair = pair + lax.dot_general(d_up, up, OVER_LAST, preferred_element_type=F32)
            pair = pair.astype(BF16)
            grad_refs[d][x] = pair[:, 0:width]
            grad_refs[d][x + 1] = pair[:, width : 2 * width]
    for c in range(0, blocks, 2):
        pair = jnp.dot(
            act, down_ref[:, c * width : (c + 2) * width], preferred_element_type=F32
        ).astype(BF16)
        out_ref[c] = pair[:, 0:width]
        out_ref[c + 1] = pair[:, width : 2 * width]


def expert(me, rows, d_act, gate, up, down, side):
    blocks, total, width = rows.shape
    hidden = gate.shape[1]
    quarter = jax.ShapeDtypeStruct((blocks // side, total, width), BF16)
    vmem = pl.BlockSpec(memory_space=pltpu.VMEM)
    return pl.pallas_call(
        expert_kernel,
        in_specs=[pl.BlockSpec(memory_space=pltpu.SMEM)] + [vmem] * 5,
        out_shape=(
            jax.ShapeDtypeStruct((total, hidden), BF16),
            jax.ShapeDtypeStruct((blocks, total, width), BF16),
        )
        + (quarter,) * side,
        compiler_params=params(),
        cost_estimate=pl.CostEstimate(
            flops=10 * total * hidden * blocks * width,
            bytes_accessed=6 * rows.size + 6 * gate.size + 6 * total * hidden,
            transcendentals=total * hidden,
        ),
        name="expert",
    )(me, rows, d_act, gate, up, down)


def down_grad_kernel(act_ref, tan_ref, grad_ref):
    grad_ref[...] = lax.dot_general(
        act_ref[...], wide_rows(tan_ref), (((0,), (0,)), ((), ())), preferred_element_type=F32
    ).astype(BF16)


def down_grad(act, tangent):
    blocks, total, width = tangent.shape
    hidden = act.shape[1]
    return pl.pallas_call(
        down_grad_kernel,
        out_shape=jax.ShapeDtypeStruct((hidden, blocks * width), BF16),
        compiler_params=params(),
        cost_estimate=pl.CostEstimate(
            flops=2 * total * hidden * blocks * width,
            bytes_accessed=2 * tangent.size + 2 * total * hidden + 2 * hidden * blocks * width,
            transcendentals=0,
        ),
        name="down_grad",
    )(act, tangent)


def half_sum_kernel(me_ref, *refs):
    count = len(refs) // 2
    for d in range(count):
        x = lax.rem(me_ref[0] + d, count)
        total = refs[0][x].astype(F32)
        for r in refs[1:count]:
            total = total + r[x].astype(F32)
        refs[count + d][...] = total.astype(BF16)


def half_sum(me, parts):
    vmem = pl.BlockSpec(memory_space=pltpu.VMEM)
    return pl.pallas_call(
        half_sum_kernel,
        in_specs=[pl.BlockSpec(memory_space=pltpu.SMEM)] + [vmem] * len(parts),
        out_shape=(jax.ShapeDtypeStruct(parts[0].shape[1:], BF16),) * len(parts),
        compiler_params=params(),
        name="half_sum",
    )(me, *parts)


def last_sum_kernel(out_ref, *refs):
    both_ref = refs[-1]
    width = out_ref.shape[2]
    total = out_ref[0].astype(F32)
    for s in range(1, out_ref.shape[0]):
        total = total + out_ref[s].astype(F32)
    both_ref[:, 0:width] = total.astype(BF16)
    total = refs[0][...].astype(F32)
    for r in refs[1:-1]:
        total = total + r[...].astype(F32)
    both_ref[:, width : 2 * width] = total.astype(BF16)


def last_sum(out_parts, grad_parts):
    _, total, width = out_parts.shape
    return pl.pallas_call(
        last_sum_kernel,
        out_shape=jax.ShapeDtypeStruct((total, 2 * width), BF16),
        compiler_params=params(),
        name="last_sum",
    )(out_parts, *grad_parts)


def combine_kernel(places_ref, weight_ref, back_ref, hid_ref, cot_ref, out_ref, grad_ref):
    block, width = hid_ref.shape
    slots = places_ref.shape[1]
    first = pl.program_id(0) * block
    where = lax.broadcasted_iota(jnp.int32, (block, slots), 0) + first
    picks = jnp.where(where == places_ref[...], 1.0, 0.0).astype(BF16)
    weighted = back_ref[:, 0:width].astype(F32) * weight_ref[...]
    high = weighted.astype(BF16)
    low = (weighted - high.astype(F32)).astype(BF16)
    terms = jnp.concatenate([high, low, back_ref[:, width : 2 * width]], axis=1)
    sums = jnp.dot(picks, terms, preferred_element_type=F32)
    combined = sums[:, 0:width] + sums[:, width : 2 * width]
    out_ref[...] = (hid_ref[...].astype(F32) + combined).astype(BF16)
    grad_ref[...] = (cot_ref[...].astype(F32) + sums[:, 2 * width : 3 * width]).astype(BF16)


def combine(places, weight, back, hidden, cotangent):
    length, width = hidden.shape
    slots = places.shape[1]
    block = 1024
    row_block = pl.BlockSpec((block, width), lambda i: (i, 0))

    def whole(shape):
        return pl.BlockSpec(shape, lambda i: (0, 0))

    return pl.pallas_call(
        combine_kernel,
        grid=(length // block,),
        in_specs=[
            whole((1, slots)),
            whole((slots, 1)),
            whole((slots, 2 * width)),
            row_block,
            row_block,
        ],
        out_specs=(row_block, row_block),
        out_shape=(jax.ShapeDtypeStruct(hidden.shape, BF16),) * 2,
        compiler_params=params(),
        name="combine",
    )(places, weight, back, hidden, cotangent)


def take_rows(array, index):
    return array.at[index].get(mode="promise_in_bounds")


def shift(block, dx, dy):
    side = SIDE
    moves = [
        (x * side + y, (x + dx) % side * side + (y + dy) % side)
        for x in range(side)
        for y in range(side)
    ]
    return lax.ppermute(block, "sp", moves)


def spread(block):
    copies = jnp.broadcast_to(block[None], (lax.axis_size("sp"),) + block.shape)
    return lax.all_to_all(copies, "sp", split_axis=0, concat_axis=0, tiled=True)


def on_device(
    queries,
    keys,
    values,
    residual,
    cotangent,
    gate_proj,
    up_proj,
    down_proj,
    chosen,
    counts,
    route_weight,
):
    rows = queries.shape[0]
    length, width = residual.shape
    places = chosen[0]
    experts = places.shape[0]
    slots = experts * SLOTS
    group = lax.axis_size("sp")
    side = SIDE
    x_groups = [[x * side + y for x in range(side)] for y in range(side)]
    y_groups = [[x * side + y for y in range(side)] for x in range(side)]
    x_me = (lax.axis_index("sp") // side).reshape(1)
    y_me = (lax.axis_index("sp") % side).reshape(1)

    packed = pack(queries, keys, values)
    qkv = lax.all_to_all(packed, "sp", split_axis=0, concat_axis=0, tiled=True)

    live = jnp.arange(SLOTS, dtype=jnp.int32)[None, :] < counts[0][:, None]
    weight = jnp.where(live, route_weight[0], jnp.float32(0.0)).reshape(slots, 1)
    flat = places.reshape(slots)
    picked_residual = take_rows(residual, flat)
    tangent = (take_rows(cotangent, flat).astype(F32) * weight).astype(BF16)
    all_tangents = lax.all_gather(tangent.reshape(experts, SLOTS, width), "ep", axis=0)
    own_tangents = lax.dynamic_index_in_dim(all_tangents, lax.axis_index("ep"), 1, False)
    owned_tangent = lax.all_gather(own_tangents.reshape(-1, width), "sp", axis=0)

    query_rows = (flat // rows) * (3 * rows) + flat % rows
    picked_queries = take_rows(qkv.reshape(-1, HD), query_rows)
    block = min(512, slots)
    picked_hidden = attention(
        picked_queries,
        pl.BlockSpec((block, HD), lambda i: (i, 0)),
        picked_residual,
        0,
        slots,
        qkv,
        block,
        "picked_attention",
    )

    def full_attention(first, count, queries_here):
        return attention(
            queries_here,
            pl.BlockSpec((2, rows, HD), lambda i: (i + first, 0, 0)),
            residual,
            first,
            count * 2 * rows,
            qkv,
            2 * rows,
            "full_attention",
        )

    owned = lax.all_to_all(
        picked_hidden.reshape(experts, SLOTS, width), "ep", split_axis=0, concat_axis=0, tiled=True
    ).reshape(-1, width)
    half = group // 4
    owned, queries_now = lax.optimization_barrier((owned, qkv))
    owned_rows = spread(owned)
    hidden_first = full_attention(0, half, queries_now)
    gate, up, down = gate_proj[0], up_proj[0], down_proj[0]
    d_act = tangent_product(owned_tangent, down)
    owned_rows, d_act, hidden_first = lax.optimization_barrier((owned_rows, d_act, hidden_first))
    act, out_part, *grad_parts = expert(y_me, owned_rows, d_act, gate, up, down, side)

    act, out_part, queries_now = lax.optimization_barrier((act, out_part, qkv))
    out_part = lax.all_to_all(
        out_part.reshape(side, -1, width),
        "sp",
        split_axis=0,
        concat_axis=0,
        axis_index_groups=x_groups,
        tiled=True,
    )
    grad_parts = [grad_parts[0]] + [shift(grad_parts[d], 0, d) for d in range(1, side)]
    grad_down = down_grad(act, owned_tangent)
    hidden_second = full_attention(half, half, queries_now)
    out_part, grad_down, hidden_second = lax.optimization_barrier(
        (out_part, grad_down, hidden_second)
    )
    out_part = jnp.sum(out_part.astype(F32).reshape(side, side, -1, width), axis=0).astype(BF16)
    out_part = lax.all_to_all(
        out_part, "sp", split_axis=0, concat_axis=0, axis_index_groups=y_groups, tiled=True
    )
    grad_parts = half_sum(x_me, grad_parts)
    grad_parts = [grad_parts[0]] + [shift(grad_parts[d], d, 0) for d in range(1, side)]
    back = last_sum(out_part, grad_parts).reshape(-1, SLOTS, 2 * width)
    back = lax.all_to_all(back, "ep", split_axis=0, concat_axis=0, tiled=True)
    block_out, grad_hidden = combine(
        flat.reshape(1, slots),
        weight,
        back.reshape(slots, 2 * width),
        jnp.concatenate([hidden_first, hidden_second], axis=0),
        cotangent,
    )
    return (block_out, grad_hidden, grad_down[None])


def solution(mesh):
    in_specs = (
        P(("ep", "sp"), None),
        P(("ep", "sp"), None),
        P(("ep", "sp"), None),
        P("ep", "sp"),
        P("ep", "sp"),
        P("ep", None, "sp"),
        P("ep", None, "sp"),
        P("ep", "sp", None),
        P("ep", None, None),
        P("ep", None),
        P("ep", None, None),
    )
    out_specs = (P("ep", "sp"), P("ep", "sp"), P("ep", "sp", None))
    return jax.shard_map(
        on_device, mesh=mesh, in_specs=in_specs, out_specs=out_specs, check_vma=False
    )
```

time: 445 us -> 227 us (0.51)
  waiting for transfers between devices: 261 us -> 59.9 us
  Pallas kernels: 0 us -> 56.5 us
  matrix products: 50.4 us -> 0 us
  other arithmetic: 31.9 us -> 5.7 us
  blocking collectives: 35.8 us -> 20.5 us
  local copies, waits for them, and re-layouts: 15.1 us -> 26.5 us
  starting transfers between devices: 35.8 us -> 41.9 us
    unnamed x6 -> x2, waiting for transfers between devices: 147 us -> 0.03 us
    pallas_call x0 -> x10, Pallas kernels: none -> 56.5 us  [the longest x3 37.4 us: attention(): pl.pallas_call(functools.partial(attention_kernel, rows), grid=(total //...]
    dot_general x23 -> x0, matrix products: 50.4 us -> none  [the longest x8 25.1 us: score_block(): jnp.einsum('hqk,khd->qhd', probs, value_heads, preferred_element_type=jnp...]
    all_gather x2, waiting for transfers between devices: 79.6 us -> 31.9 us  [the longest x1 31.9 us: on_device(): lax.all_gather(tangent.reshape(experts, SLOTS, width), 'ep', axis=0)]
    all_to_all x2 -> x1, blocking collectives: 35.8 us -> 20.5 us  [on_device(): lax.all_to_all(picked_hidden.reshape(experts, SLOTS, width), 'ep', split_...]
    scatter-add x2 -> x0, other arithmetic: 10.6 us -> none  [the longest x1 6.15 us: on_device(): combined = jnp.zeros((length, col_width), jnp.float32).at[flat_places].ad...]
    all_to_all x5, waiting for transfers between devices: 33.9 us -> 24 us  [the longest x1 10.5 us: on_device(): back = lax.all_to_all(back, 'ep', split_axis=0, concat_axis=0, tiled=True)]
    ppermute x0 -> x6, starting transfers between devices: none -> 9.17 us  [shift(): return lax.ppermute(block, 'sp', moves)]
  transfers between devices with their start and end apart: 9 -> 13, of which waited for: 7 -> 7; matrix products, arithmetic and copies ran while one was open for 8% -> 5% of each run, Pallas kernels for 0% -> 20%
where the time goes in v1:
time: 227 us; the launch traced here: 225 us
  waiting for transfers between devices  59.9 us (26%)
  Pallas kernels  56.5 us (25%)
  starting transfers between devices  41.9 us (18%)
  local copies, waits for them, and re-layouts  26.5 us (12%)
  blocking collectives  20.5 us (9%)
  between operations  14.3 us (6%)
  other arithmetic  5.7 us (3%)
    pallas_call x3, Pallas kernels, attention(): pl.pallas_call(functools.partial(attention_kernel, rows), grid=(total //...  37.4 us
    all_gather x1, waiting for transfers between devices, on_device(): lax.all_gather(tangent.reshape(experts, SLOTS, width), 'ep', axis=0)  31.9 us
    all_to_all x1, blocking collectives, on_device(): lax.all_to_all(picked_hidden.reshape(experts, SLOTS, width), 'ep', split_...  20.5 us
    unnamed x44, local copies, waits for them, and re-layouts  15.7 us
    all_to_all x1, waiting for transfers between devices, on_device(): back = lax.all_to_all(back, 'ep', split_axis=0, concat_axis=0, tiled=True)  10.5 us
    all_to_all x1, waiting for transfers between devices, spread(): return lax.all_to_all(copies, 'sp', split_axis=0, concat_axis=0, tiled=True)  9.23 us
    ppermute x6, starting transfers between devices, shift(): return lax.ppermute(block, 'sp', moves)  9.17 us
    all_to_all x1, starting transfers between devices, on_device(): back = lax.all_to_all(back, 'ep', split_axis=0, concat_axis=0, tiled=True)  7.86 us
  transfers between devices with their start and end apart: 13, of which 7 were waited for; matrix products, arithmetic and copies ran while one was open for 5% of the time, Pallas kernels for 20%

profile of v1, /device:TPU:1, one launch (start us, length us, event | category | flops | bytes accessed | tf_op | source)
XLA Modules:
  0.0 225.3 jit_solution(8418289127516211556)
XLA Ops:
  7.2 0.8 reshape_squeeze.3
  8.0 2.4 %gather_fusion.2 = bf16[512,128]{1,0:T(8,128)(2,1)S(1)} fusion(bf16[4096,128]{1,0:T(8,128)(2,1)} %cot_ref.1, s32[1024]{0:T(1024)S(1)} %pad_clamp_fusion), kind=kCustom, calls=%fused_computation.2 | custom fusion | bytes 264192 | tf_op jit(solution)/shard_map/gather | solution.py:332
  11.2 0.8 fusion
  12.0 4.4 %pack_qkv.1 = bf16[16,768,128]{2,1,0:T(8,128)(2,1)} custom-call(bf16[256,2048]{1,0:T(8,128)(2,1)} %q_ref.1, bf16[256,2048]{1,0:T(8,128)(2,1)} %k_ref.1, bf16[256,2048]{1,0:T(8,128)(2,1)} %v_ref.1), custom_call_target="tpu_custom_call" | custom-call | tf_op jit(solution)/shard_map/pack_qkv/pallas_call | solution.py:40
  16.4 7.6 %all-to-all-start = ((bf16[16,768,128]{2,1,0:T(8,128)(2,1)}), bf16[16,768,128]{2,1,0:T(8,128)(2,1)S(1)}, u32[]{:S(2)}, u32[]{:S(2)}) async-start(bf16[16,768,128]{2,1,0:T(8,128)(2,1)} %pack_qkv.1), calls=%async_computation | async-start | bytes 6291456 | tf_op jit(solution)/shard_map/all_to_all | solution.py:376
  24.0 31.9 %all-gather.3.cloned.1.call-done = bf16[16,16,32,128]{3,2,1,0:T(8,128)(2,1)} async-done(((bf16[1,16,32,128]{3,2,1,0:T(8,128)(2,1)}), bf16[16,16,32,128]{3,2,1,0:T(8,128)(2,1)}) %all-gather.3.cloned.1.call-update) | async-done | bytes 2097168 | tf_op jit(solution)/shard_map/all_gather | solution.py:383
  56.0 1.6 constant_dynamic-slice_fusion
  57.6 2.4 %gather_fusion.1 = bf16[512,128]{1,0:T(8,128)(2,1)S(1)} fusion(bf16[4096,128]{1,0:T(8,128)(2,1)} %res_ref.3, s32[1024]{0:T(1024)S(1)} %pad_clamp_fusion), kind=kCustom, calls=%fused_computation.1 | custom fusion | bytes 264192 | tf_op jit(solution)/shard_map/gather | solution.py:332
  60.0 4.3 %all-to-all-done.qkv_ref.q_ref = bf16[16,768,128]{2,1,0:T(8,128)(2,1)S(1)} async-done(((bf16[16,768,128]{2,1,0:T(8,128)(2,1)}), bf16[16,768,128]{2,1,0:T(8,128)(2,1)S(1)}, u32[]{:S(2)}, u32[]{:S(2)}) %all-to-all-start) | async-done | bytes 3145760 | tf_op jit(solution)/shard_map/all_to_all | solution.py:376
  64.3 1.3 gather_fusion
  65.6 4.5 %picked_attention.1 = bf16[512,128]{1,0:T(8,128)(2,1)S(1)} custom-call(bf16[512,128]{1,0:T(8,128)(2,1)S(1)} %gather_fusion, bf16[512,128]{1,0:T(8,128)(2,1)S(1)} %gather_fusion.1, bf16[16,768,128]{2,1,0:T(8,128)(2,1)S(1)} %all-to-all-done.qkv_ref.q_ref), custom_call_target="tpu_custom_call" | custom-call | flops 2147483648 | bytes 3670016 | tf_op jit(solution)/shard_map/picked_attention/pallas_call | solution.py:118
  70.1 20.5 %all_to_all.30 = bf16[16,32,128]{2,1,0:T(8,128)(2,1)S(1)} all-to-all(bf16[16,32,128]{2,1,0:T(8,128)(2,1)S(1)} %bitcast.25), channel_id=1, replica_groups=mesh['ep'=16,'sp'=16] {'ep'}, dimensions={0} | all-to-all | bytes 262144 | tf_op jit(solution)/shard_map/all_to_all | solution.py:413
  90.7 1.8 broadcast_in_dim.20
  92.4 7.6 %all-to-all-start.2 = ((bf16[16,512,128]{2,1,0:T(8,128)(2,1)}), bf16[16,512,128]{2,1,0:T(8,128)(2,1)}, u32[]{:S(2)}, u32[]{:S(2)}) async-start(bf16[16,512,128]{2,1,0:T(8,128)(2,1)} %broadcast_in_dim.20), calls=%async_computation.2 | async-start | bytes 4194304 | tf_op jit(solution)/shard_map/all_to_all | solution.py:347
  100.1 1.2 copy-done.5
  101.3 16.5 %full_attention.2 = bf16[2048,128]{1,0:T(8,128)(2,1)S(1)} custom-call(bf16[16,768,128]{2,1,0:T(8,128)(2,1)S(1)} %all-to-all-done.qkv_ref.q_ref, bf16[4096,128]{1,0:T(8,128)(2,1)S(1)} %copy-done.5, bf16[16,768,128]{2,1,0:T(8,128)(2,1)S(1)} %all-to-all-done.qkv_ref.q_ref), custom_call_target="tpu_custom_call" | custom-call | flops 8589934592 | bytes 5242880 | tf_op jit(solution)/shard_map/full_attention/pallas_call | solution.py:118
  117.8 0.8 copy-done.11
  118.6 1.6 copy-done
  120.2 1.2 copy-done.3
  122.2 0.8 copy-done.9
  122.9 9.2 %all-to-all-done.2.x_ref = bf16[16,512,128]{2,1,0:T(8,128)(2,1)} async-done(((bf16[16,512,128]{2,1,0:T(8,128)(2,1)}), bf16[16,512,128]{2,1,0:T(8,128)(2,1)}, u32[]{:S(2)}, u32[]{:S(2)}) %all-to-all-start.2) | async-done | bytes 2097184 | tf_op jit(solution)/shard_map/all_to_all | solution.py:347
  132.2 1.2 copy-done.4
  133.4 1.0 copy-done.10
  134.5 1.2 copy-done.14
  135.7 1.2 copy-done.15
  136.9 5.9 %expert.1 = (bf16[512,256]{1,0:T(8,128)(2,1)S(1)}, bf16[16,512,128]{2,1,0:T(8,128)(2,1)}, bf16[4,512,128]{2,1,0:T(8,128)(2,1)S(1)}, bf16[4,512,128]{2,1,0:T(8,12...) custom-call(s32[1]{0:T(128)} %bitcast.1.me_ref, ...), custom_call_target="tpu_custom_call" | custom-call | flops 2684354560 | bytes 10223616 | tf_op jit(solution)/shard_map/expert/pallas_call | solution.py:205
  142.8 0.8 copy-done.7
  143.6 0.8 copy-done.16
  144.5 0.8 copy-done.18
  145.3 0.8 copy-done.17
  146.1 4.4 %all-to-all-start.3 = ((bf16[4,2048,128]{2,1,0:T(8,128)(2,1)}), bf16[4,2048,128]{2,1,0:T(8,128)(2,1)}, u32[]{:S(2)}, u32[]{:S(2)}) async-start(bf16[4,2048,128]{2,1,0:T(8,128)(2,1)} %bitcast.28), calls=%async_computation.3 | async-start | bytes 4194304 | tf_op jit(solution)/shard_map/all_to_all | solution.py:426
  150.9 3.9 %collective-permute-start.1 = (bf16[4,512,128]{2,1,0:T(8,128)(2,1)}, bf16[4,512,128]{2,1,0:T(8,128)(2,1)}, u32[]{:S(2)}, u32[]{:S(2)}) collective-permute-start(bf16[4,512,128]{2,1,0:T(8,128)(2,1)} %copy-done.17), channel_id=1, source_target_pairs={{0,2},{1,3},{2,0},{3,1},{4,6},{5,7},{6,4},{7,5},{8,10},{9,11},{10,... | collective-permute-start | bytes 1572872 | tf_op jit(solution)/shard_map/ppermute | solution.py:342
  154.8 1.3 collective-permute-start.2
  156.2 1.2 copy-done.6
  157.4 16.4 %full_attention.3 = bf16[2048,128]{1,0:T(8,128)(2,1)S(1)} custom-call(bf16[16,768,128]{2,1,0:T(8,128)(2,1)S(1)} %all-to-all-done.qkv_ref.q_ref, bf16[4096,128]{1,0:T(8,128)(2,1)S(1)} %copy-done.6, bf16[16,768,128]{2,1,0:T(8,128)(2,1)S(1)} %all-to-all-done.qkv_ref.q_ref), custom_call_target="tpu_custom_call" | custom-call | flops 8589934592 | bytes 5242880 | tf_op jit(solution)/shard_map/full_attention/pallas_call | solution.py:118
  173.8 0.8 copy-done.13
  174.7 1.7 down_grad.1
  176.4 2.9 %reduce_sum.12 = bf16[2048,128]{1,0:T(8,128)(2,1)} reduce(bf16[4,2048,128]{2,1,0:T(8,128)(2,1)} %all-to-all-done.3, bf16[]{:T(256)} %constant.72.clone.1), dimensions={0}, to_apply=%region_0.1 | reduce | flops 786432 | bytes 2621442 | tf_op jit(solution)/shard_map/reduce_sum | solution.py:440
  179.3 5.1 %all-to-all-start.4 = ((bf16[4,512,128]{2,1,0:T(8,128)(2,1)}), bf16[4,512,128]{2,1,0:T(8,128)(2,1)S(1)}, u32[]{:S(2)}, u32[]{:S(2)}) async-start(bf16[4,512,128]{2,1,0:T(8,128)(2,1)} %bitcast.14), calls=%async_computation.4 | async-start | bytes 1048576 | tf_op jit(solution)/shard_map/all_to_all | solution.py:441
  184.7 1.7 half_sum.1
  186.7 2.0 collective-permute-start.4
  188.7 1.2 collective-permute-start.5
  190.3 2.7 %collective-permute-done.3.refs_1_ = bf16[512,128]{1,0:T(8,128)(2,1)S(1)} collective-permute-done((bf16[512,128]{1,0:T(8,128)(2,1)S(1)}, bf16[512,128]{1,0:T(8,128)(2,1)S(1)}, u32[]{:S(2)}, u32[]{:S(2)}) %collective-permute-start.3) | collective-permute-done | bytes 131104 | tf_op jit(solution)/shard_map/ppermute | solution.py:342
  194.2 0.8 last_sum.1
  195.0 7.9 %all-to-all-start.5 = ((bf16[16,32,256]{2,1,0:T(8,128)(2,1)}), bf16[16,32,256]{2,1,0:T(8,128)(2,1)S(1)}, u32[]{:S(2)}, u32[]{:S(2)}) async-start(bf16[16,32,256]{2,1,0:T(8,128)(2,1)} %bitcast.16), calls=%async_computation.5 | async-start | bytes 524288 | tf_op jit(solution)/shard_map/all_to_all | solution.py:447
  203.0 1.1 pad_maximum_fusion.hid_ref
  204.1 10.5 %all-to-all-done.5 = bf16[16,32,256]{2,1,0:T(8,128)(2,1)S(1)} async-done(((bf16[16,32,256]{2,1,0:T(8,128)(2,1)}), bf16[16,32,256]{2,1,0:T(8,128)(2,1)S(1)}, u32[]{:S(2)}, u32[]{:S(2)}) %all-to-all-start.5) | async-done | bytes 262176 | tf_op jit(solution)/shard_map/all_to_all | solution.py:447
  214.6 3.8 %combine.1 = (bf16[4096,128]{1,0:T(8,128)(2,1)}, bf16[4096,128]{1,0:T(8,128)(2,1)}) custom-call(s32[1,512]{1,0:T(1,128)S(1)} %reshape_reshape_squeeze.3.places_ref, f32[512,1]{1,0:T(8,128)S(1)} %broadcast_select_fusion.weight_ref, bf16[512,256]{1,0:T(8,128)(2,1)S(1)} %bitcast.24, bf16[4096,128]{1,0:T(8,128)(2,1)S(1)} %pad_maximum_fusion.hid_ref, ...), custom_call_target="tpu_custom_call" | custom-call | tf_op jit(solution)/shard_map/combine/pallas_call | solution.py:314
  (53 shorter events, 4.4 us)
Async XLA Ops:
  7.2 48.8 %all-gather.3.cloned.1.call-start = ((), (), s32[]{:S(2)}) async-start(), calls=%async_computation.6 | async-start | bytes 2228224 | tf_op jit(solution)/shard_map/all_gather | solution.py:383
  16.4 47.9 %all-to-all-start = ((bf16[16,768,128]{2,1,0:T(8,128)(2,1)}), bf16[16,768,128]{2,1,0:T(8,128)(2,1)S(1)}, u32[]{:S(2)}, u32[]{:S(2)}) async-start(bf16[16,768,128]{2,1,0:T(8,128)(2,1)} %pack_qkv.1), calls=%async_computation | async-start | bytes 6291456 | tf_op jit(solution)/shard_map/all_to_all | solution.py:376
  24.0 94.6 %all-gather.5.cloned.1.call-start = ((), (), s32[]{:S(2)}) async-start(), calls=%async_computation.7 | async-start | bytes 2228224 | tf_op jit(solution)/shard_map/all_gather | solution.py:385
  92.4 39.8 %all-to-all-start.2 = ((bf16[16,512,128]{2,1,0:T(8,128)(2,1)}), bf16[16,512,128]{2,1,0:T(8,128)(2,1)}, u32[]{:S(2)}, u32[]{:S(2)}) async-start(bf16[16,512,128]{2,1,0:T(8,128)(2,1)} %broadcast_in_dim.20), calls=%async_computation.2 | async-start | bytes 4194304 | tf_op jit(solution)/shard_map/all_to_all | solution.py:347
  100.1 1.2 copy-start.5
  117.8 0.8 copy-start.11
  118.6 1.6 copy-start
  120.2 1.2 copy-start.3
  122.2 0.8 copy-start.9
  132.2 1.2 copy-start.4
  133.4 1.0 copy-start.10
  134.5 1.2 copy-start.14
  135.7 1.2 copy-start.15
  142.8 0.8 copy-start.7
  143.6 0.8 copy-start.16
  144.5 0.8 copy-start.18
  145.3 0.8 copy-start.17
  146.1 30.3 %all-to-all-start.3 = ((bf16[4,2048,128]{2,1,0:T(8,128)(2,1)}), bf16[4,2048,128]{2,1,0:T(8,128)(2,1)}, u32[]{:S(2)}, u32[]{:S(2)}) async-start(bf16[4,2048,128]{2,1,0:T(8,128)(2,1)} %bitcast.28), calls=%async_computation.3 | async-start | bytes 4194304 | tf_op jit(solution)/shard_map/all_to_all | solution.py:426
  150.5 34.1 %collective-permute-start = (bf16[4,512,128]{2,1,0:T(8,128)(2,1)}, bf16[4,512,128]{2,1,0:T(8,128)(2,1)}, u32[]{:S(2)}, u32[]{:S(2)}) collective-permute-start(bf16[4,512,128]{2,1,0:T(8,128)(2,1)} %copy-done.18), channel_id=1, source_target_pairs={{0,1},{1,2},{2,3},{3,0},{4,5},{5,6},{6,7},{7,4},{8,9},{9,10},{10,1... | collective-permute-start | bytes 1572872 | tf_op jit(solution)/shard_map/ppermute | solution.py:342
  150.9 33.7 %collective-permute-start.1 = (bf16[4,512,128]{2,1,0:T(8,128)(2,1)}, bf16[4,512,128]{2,1,0:T(8,128)(2,1)}, u32[]{:S(2)}, u32[]{:S(2)}) collective-permute-start(bf16[4,512,128]{2,1,0:T(8,128)(2,1)} %copy-done.17), channel_id=1, source_target_pairs={{0,2},{1,3},{2,0},{3,1},{4,6},{5,7},{6,4},{7,5},{8,10},{9,11},{10,... | collective-permute-start | bytes 1572872 | tf_op jit(solution)/shard_map/ppermute | solution.py:342
  154.8 19.8 %copy-start.1 = (bf16[16,512,128]{2,1,0:T(8,128)(2,1)S(1)}, bf16[16,512,128]{2,1,0:T(8,128)(2,1)}, u32[]{:S(2)}) copy-start(bf16[16,512,128]{2,1,0:T(8,128)(2,1)} %all-gather.5.cloned.1.call-done.tan_ref) | copy-start | bytes 6291460
  154.8 29.8 %collective-permute-start.2 = (bf16[4,512,128]{2,1,0:T(8,128)(2,1)}, bf16[4,512,128]{2,1,0:T(8,128)(2,1)}, u32[]{:S(2)}, u32[]{:S(2)}) collective-permute-start(bf16[4,512,128]{2,1,0:T(8,128)(2,1)} %copy-done.16), channel_id=1, source_target_pairs={{0,3},{1,0},{2,1},{3,2},{4,7},{5,4},{6,5},{7,6},{8,11},{9,8},{10,9... | collective-permute-start | bytes 1572872 | tf_op jit(solution)/shard_map/ppermute | solution.py:342
  156.2 1.2 copy-start.6
  173.8 0.8 copy-start.13
  176.4 8.0 %copy-start.19 = (f32[1,16,32]{2,1,0:T(8,128)S(1)}, f32[1,16,32]{2,1,0:T(8,128)}, u32[]{:S(2)}) copy-start(f32[1,16,32]{2,1,0:T(8,128)} %param.21) | copy-start | bytes 6148
  176.4 8.3 %copy-start.8 = (bf16[4,512,128]{2,1,0:T(8,128)(2,1)S(1)}, bf16[4,512,128]{2,1,0:T(8,128)(2,1)}, u32[]{:S(2)}) copy-start(bf16[4,512,128]{2,1,0:T(8,128)(2,1)} %copy-done.7) | copy-start | bytes 1572868
  179.3 10.7 %copy-start.21 = (s32[1,16]{1,0:T(1,128)S(1)}, s32[1,16]{1,0:T(1,128)}, u32[]{:S(2)}) copy-start(s32[1,16]{1,0:T(1,128)} %param.20) | copy-start | bytes 196
  179.3 14.9 %all-to-all-start.4 = ((bf16[4,512,128]{2,1,0:T(8,128)(2,1)}), bf16[4,512,128]{2,1,0:T(8,128)(2,1)S(1)}, u32[]{:S(2)}, u32[]{:S(2)}) async-start(bf16[4,512,128]{2,1,0:T(8,128)(2,1)} %bitcast.14), calls=%async_computation.4 | async-start | bytes 1048576 | tf_op jit(solution)/shard_map/all_to_all | solution.py:441
  184.6 18.3 %copy-start.20 = (s32[1,16,32]{2,1,0:T(8,128)S(1)}, s32[1,16,32]{2,1,0:T(8,128)}, u32[]{:S(2)}) copy-start(s32[1,16,32]{2,1,0:T(8,128)} %param.19) | copy-start | bytes 6148
  184.7 18.4 %copy-start.12 = (bf16[2048,128]{1,0:T(8,128)(2,1)S(1)}, bf16[2048,128]{1,0:T(8,128)(2,1)}, u32[]{:S(2)}) copy-start(bf16[2048,128]{1,0:T(8,128)(2,1)} %copy-done.11) | copy-start | bytes 1572868
  186.3 6.7 %collective-permute-start.3 = (bf16[512,128]{1,0:T(8,128)(2,1)S(1)}, bf16[512,128]{1,0:T(8,128)(2,1)S(1)}, u32[]{:S(2)}, u32[]{:S(2)}) collective-permute-start(bf16[512,128]{1,0:T(8,128)(2,1)S(1)} %get-tuple-element.41), channel_id=1, source_target_pairs={{0,4},{1,5},{2,6},{3,7},{4,8},{5,9},{6,10},{7,11},{8,12},{9,13},{1... | collective-permute-start | bytes 393224 | tf_op jit(solution)/shard_map/ppermute | solution.py:342
  186.7 6.8 %collective-permute-start.4 = (bf16[512,128]{1,0:T(8,128)(2,1)S(1)}, bf16[512,128]{1,0:T(8,128)(2,1)S(1)}, u32[]{:S(2)}, u32[]{:S(2)}) collective-permute-start(bf16[512,128]{1,0:T(8,128)(2,1)S(1)} %get-tuple-element.42), channel_id=1, source_target_pairs={{0,8},{1,9},{2,10},{3,11},{4,12},{5,13},{6,14},{7,15},{8,0},{9,1},... | collective-permute-start | bytes 393224 | tf_op jit(solution)/shard_map/ppermute | solution.py:342
  188.7 5.4 %collective-permute-start.5 = (bf16[512,128]{1,0:T(8,128)(2,1)S(1)}, bf16[512,128]{1,0:T(8,128)(2,1)S(1)}, u32[]{:S(2)}, u32[]{:S(2)}) collective-permute-start(bf16[512,128]{1,0:T(8,128)(2,1)S(1)} %get-tuple-element.43), channel_id=1, source_target_pairs={{0,12},{1,13},{2,14},{3,15},{4,0},{5,1},{6,2},{7,3},{8,4},{9,5},{1... | collective-permute-start | bytes 393224 | tf_op jit(solution)/shard_map/ppermute | solution.py:342
  194.2 20.4 %copy-start.2 = (bf16[4096,128]{1,0:T(8,128)(2,1)S(1)}, bf16[4096,128]{1,0:T(8,128)(2,1)}, u32[]{:S(2)}) copy-start(bf16[4096,128]{1,0:T(8,128)(2,1)} %cot_ref.1) | copy-start | bytes 3145732
  195.0 19.6 %all-to-all-start.5 = ((bf16[16,32,256]{2,1,0:T(8,128)(2,1)}), bf16[16,32,256]{2,1,0:T(8,128)(2,1)S(1)}, u32[]{:S(2)}, u32[]{:S(2)}) async-start(bf16[16,32,256]{2,1,0:T(8,128)(2,1)} %bitcast.16), calls=%async_computation.5 | async-start | bytes 524288 | tf_op jit(solution)/shard_map/all_to_all | solution.py:447
Sparse Core Ops, SparseCore 0:
  12.2 43.7 all-gather.2
  59.0 52.5 all-gather.4

commit v2 on v1

--- a/solution.py
+++ b/solution.py
@@ -23,26 +23,48 @@
     return pltpu.CompilerParams(vmem_limit_bytes=limit)
 
 
-def pack_kernel(q_ref, k_ref, v_ref, out_ref):
-    rows, width = q_ref.shape
-    for h in range(width // HD):
-        here = slice(h * HD, (h + 1) * HD)
-        out_ref[h, 0:rows, :] = q_ref[:, here]
-        out_ref[h, rows : 2 * rows, :] = k_ref[:, here]
-        out_ref[h, 2 * rows : 3 * rows, :] = v_ref[:, here]
+def pack_kernel(q_hbm, k_hbm, v_hbm, out_hbm, stage_ref, in_sems, out_sems):
+    rows, width = q_hbm.shape
+    heads = width // HD
+    sources = (q_hbm, k_hbm, v_hbm)
+    loads = []
+    for h in range(heads):
+        for i, ref in enumerate(sources):
+            loads.append(
+                pltpu.make_async_copy(
+                    ref.at[:, pl.ds(h * HD, HD)],
+                    stage_ref.at[h, pl.ds(i * rows, rows), :],
+                    in_sems.at[3 * h + i],
+                )
+            )
+    for copy in loads:
+        copy.start()
+    stores = [
+        pltpu.make_async_copy(stage_ref.at[h], out_hbm.at[h], out_sems.at[h]) for h in range(heads)
+    ]
+    for h in range(heads):
+        for copy in loads[3 * h : 3 * h + 3]:
+            copy.wait()
+        stores[h].start()
+    for copy in stores:
+        copy.wait()
 
 
 def pack(queries, keys, values):
     rows, width = queries.shape
     heads = width // HD
-    steps = 4
-    columns = pl.BlockSpec((rows, width // steps), lambda h: (0, h))
+    shape = (heads, 3 * rows, HD)
+    hbm = pl.BlockSpec(memory_space=pltpu.HBM)
     return pl.pallas_call(
         pack_kernel,
-        grid=(steps,),
-        in_specs=[columns] * 3,
-        out_specs=pl.BlockSpec((heads // steps, 3 * rows, HD), lambda h: (h, 0, 0)),
-        out_shape=jax.ShapeDtypeStruct((heads, 3 * rows, HD), BF16),
+        in_specs=[hbm] * 3,
+        out_specs=hbm,
+        out_shape=jax.ShapeDtypeStruct(shape, BF16),
+        scratch_shapes=[
+            pltpu.VMEM(shape, BF16),
+            pltpu.SemaphoreType.DMA((3 * heads,)),
+            pltpu.SemaphoreType.DMA((heads,)),
+        ],
         compiler_params=params(BIG_VMEM),
         name="pack_qkv",
     )(queries, keys, values)
@@ -162,22 +184,72 @@
     )(tangent, down)
 
 
+def in_pieces(src, dst, sems, first, pieces=4):
+    rows = src.shape[0] // pieces
+    return [
+        pltpu.make_async_copy(
+            src.at[pl.ds(i * rows, rows)], dst.at[pl.ds(i * rows, rows)], sems.at[first + i]
+        )
+        for i in range(pieces)
+    ]
+
+
 def expert_kernel(
-    me_ref, x_ref, d_act_ref, gate_ref, up_ref, down_ref, act_ref, out_ref, *grad_refs
+    me_ref, x_hbm, d_act_hbm, gate_hbm, up_hbm, down_hbm, act_hbm, out_hbm, *rest
 ):
-    rows = wide_rows(x_ref)
+    *grad_hbm, x_ref, d_act_ref, gate_ref, up_ref, down_ref, act_ref = rest[:-4]
+    out_ref, stage_ref, in_sems, out_sems = rest[-4:]
+    side, _, _, _, width = x_hbm.shape
+    blocks = side * side
+    load_x = [
+        pltpu.make_async_copy(
+            x_hbm.at[c // side, :, c % side],
+            x_ref.at[:, :, pl.ds(c * width, width)],
+            in_sems.at[12 + c],
+        )
+        for c in range(blocks)
+    ]
+    load_gate = in_pieces(gate_hbm, gate_ref, in_sems, 0)
+    load_up = in_pieces(up_hbm, up_ref, in_sems, 4)
+    load_d_act = in_pieces(d_act_hbm, d_act_ref, in_sems, 8)
+    load_down = in_pieces(down_hbm, down_ref, in_sems, 12 + blocks)
+    for copy in load_gate + load_x + load_up + load_down + load_d_act:
+        copy.start()
+    for copy in load_gate + load_x:
+        copy.wait()
+    rows = x_ref[...].reshape(act_ref.shape[0], blocks * width)
     gate_pre = jnp.dot(rows, gate_ref[...], preferred_element_type=F32)
+    for copy in load_up:
+        copy.wait()
     up_pre = jnp.dot(rows, up_ref[...], preferred_element_type=F32)
     sig = jax.nn.sigmoid(gate_pre)
     silu = gate_pre * sig
     act = (silu * up_pre).astype(BF16)
     act_ref[...] = act
+    stores = in_pieces(act_ref, act_hbm, out_sems, 4 * side)
+    for copy in stores:
+        copy.start()
+    for copy in load_down:
+        copy.wait()
+    for c in range(0, blocks, 2):
+        pair = jnp.dot(
+            act, down_ref[:, c * width : (c + 2) * width], preferred_element_type=F32
+        ).astype(BF16)
+        out_ref[c] = pair[:, 0:width]
+        out_ref[c + 1] = pair[:, width : 2 * width]
+        here = pl.ds(c, 2)
+        stores.append(
+            pltpu.make_async_copy(
+                out_ref.at[here], out_hbm.at[here], out_sems.at[4 * side + 4 + c // 2]
+            )
+        )
+        stores[-1].start()
+    for copy in load_d_act:
+        copy.wait()
     d_act = d_act_ref[...]
     d_gate = (d_act * up_pre * sig * (1.0 + gate_pre * (1.0 - sig))).astype(BF16)
     d_up = (d_act * silu).astype(BF16)
-    blocks, _, width = out_ref.shape
-    side = len(grad_refs)
-    for d in range(side):
+    for d in list(range(1, side)) + [0]:
         y = lax.rem(me_ref[0] + d, side)
         for x in range(0, side, 2):
             first = pl.ds(pl.multiple_of((x * side + y) * width, width), width)
@@ -187,33 +259,48 @@
             pair = lax.dot_general(d_gate, gate, OVER_LAST, preferred_element_type=F32)
             pair = pair + lax.dot_general(d_up, up, OVER_LAST, preferred_element_type=F32)
             pair = pair.astype(BF16)
-            grad_refs[d][x] = pair[:, 0:width]
-            grad_refs[d][x + 1] = pair[:, width : 2 * width]
-    for c in range(0, blocks, 2):
-        pair = jnp.dot(
-            act, down_ref[:, c * width : (c + 2) * width], preferred_element_type=F32
-        ).astype(BF16)
-        out_ref[c] = pair[:, 0:width]
-        out_ref[c + 1] = pair[:, width : 2 * width]
-
-
-def expert(me, rows, d_act, gate, up, down, side):
-    blocks, total, width = rows.shape
+            stage_ref[d, x] = pair[:, 0:width]
+            stage_ref[d, x + 1] = pair[:, width : 2 * width]
+        here = in_pieces(stage_ref.at[d], grad_hbm[d], out_sems, 4 * d)
+        for copy in here:
+            copy.start()
+        stores += here
+    for copy in stores:
+        copy.wait()
+
+
+def expert(me, rows, d_act, gate, up, down):
+    side, images, _, slots, width = rows.shape
+    blocks = side * side
+    total = images * slots
     hidden = gate.shape[1]
     quarter = jax.ShapeDtypeStruct((blocks // side, total, width), BF16)
-    vmem = pl.BlockSpec(memory_space=pltpu.VMEM)
+    hbm = pl.BlockSpec(memory_space=pltpu.HBM)
     return pl.pallas_call(
         expert_kernel,
-        in_specs=[pl.BlockSpec(memory_space=pltpu.SMEM)] + [vmem] * 5,
+        in_specs=[pl.BlockSpec(memory_space=pltpu.SMEM)] + [hbm] * 5,
+        out_specs=(hbm,) * (side + 2),
         out_shape=(
             jax.ShapeDtypeStruct((total, hidden), BF16),
             jax.ShapeDtypeStruct((blocks, total, width), BF16),
         )
         + (quarter,) * side,
-        compiler_params=params(),
+        scratch_shapes=[
+            pltpu.VMEM((images, slots, blocks * width), BF16),
+            pltpu.VMEM(d_act.shape, F32),
+            pltpu.VMEM(gate.shape, BF16),
+            pltpu.VMEM(up.shape, BF16),
+            pltpu.VMEM(down.shape, BF16),
+            pltpu.VMEM((total, hidden), BF16),
+            pltpu.VMEM((blocks, total, width), BF16),
+            pltpu.VMEM((side,) + quarter.shape, BF16),
+            pltpu.SemaphoreType.DMA((16 + blocks,)),
+            pltpu.SemaphoreType.DMA((4 * side + 4 + blocks // 2,)),
+        ],
+        compiler_params=params(BIG_VMEM),
         cost_estimate=pl.CostEstimate(
             flops=10 * total * hidden * blocks * width,
-            bytes_accessed=6 * rows.size + 6 * gate.size + 6 * total * hidden,
+            bytes_accessed=4 * rows.size + 4 * gate.size + 6 * total * hidden,
             transcendentals=total * hidden,
         ),
         name="expert",
@@ -221,8 +308,9 @@
 
 
 def down_grad_kernel(act_ref, tan_ref, grad_ref):
+    tangent = wide_rows(tan_ref)
     grad_ref[...] = lax.dot_general(
-        act_ref[...], wide_rows(tan_ref), (((0,), (0,)), ((), ())), preferred_element_type=F32
+        act_ref[...], tangent, (((0,), (0,)), ((), ())), preferred_element_type=F32
     ).astype(BF16)
 
 
@@ -240,6 +328,23 @@
         ),
         name="down_grad",
     )(act, tangent)
+
+
+def quarter_sum_kernel(in_ref, out_ref):
+    for b in range(out_ref.shape[0]):
+        total = in_ref[0, b].astype(F32)
+        for s in range(1, in_ref.shape[0]):
+            total = total + in_ref[s, b].astype(F32)
+        out_ref[b] = total.astype(BF16)
+
+
+def quarter_sum(parts):
+    return pl.pallas_call(
+        quarter_sum_kernel,
+        out_shape=jax.ShapeDtypeStruct(parts.shape[1:], BF16),
+        compiler_params=params(),
+        name="quarter_sum",
+    )(parts)
 
 
 def half_sum_kernel(me_ref, *refs):
@@ -293,13 +398,10 @@
     where = lax.broadcasted_iota(jnp.int32, (block, slots), 0) + first
     picks = jnp.where(where == places_ref[...], 1.0, 0.0).astype(BF16)
     weighted = back_ref[:, 0:width].astype(F32) * weight_ref[...]
-    high = weighted.astype(BF16)
-    low = (weighted - high.astype(F32)).astype(BF16)
-    terms = jnp.concatenate([high, low, back_ref[:, width : 2 * width]], axis=1)
+    terms = jnp.concatenate([weighted.astype(BF16), back_ref[:, width : 2 * width]], axis=1)
     sums = jnp.dot(picks, terms, preferred_element_type=F32)
-    combined = sums[:, 0:width] + sums[:, width : 2 * width]
-    out_ref[...] = (hid_ref[...].astype(F32) + combined).astype(BF16)
-    grad_ref[...] = (cot_ref[...].astype(F32) + sums[:, 2 * width : 3 * width]).astype(BF16)
+    out_ref[...] = (hid_ref[...].astype(F32) + sums[:, 0:width]).astype(BF16)
+    grad_ref[...] = (cot_ref[...].astype(F32) + sums[:, width : 2 * width]).astype(BF16)
 
 
 def combine(places, weight, back, hidden, cotangent):
@@ -340,11 +442,6 @@
         for y in range(side)
     ]
     return lax.ppermute(block, "sp", moves)
-
-
-def spread(block):
-    copies = jnp.broadcast_to(block[None], (lax.axis_size("sp"),) + block.shape)
-    return lax.all_to_all(copies, "sp", split_axis=0, concat_axis=0, tiled=True)
 
 
 def on_device(
@@ -373,16 +470,20 @@
     y_me = (lax.axis_index("sp") % side).reshape(1)
 
     packed = pack(queries, keys, values)
+    packed, cotangent_now, residual_now, flat, counts, route_weight = lax.optimization_barrier(
+        (packed, cotangent, residual, places.reshape(slots), counts, route_weight)
+    )
     qkv = lax.all_to_all(packed, "sp", split_axis=0, concat_axis=0, tiled=True)
 
     live = jnp.arange(SLOTS, dtype=jnp.int32)[None, :] < counts[0][:, None]
     weight = jnp.where(live, route_weight[0], jnp.float32(0.0)).reshape(slots, 1)
-    flat = places.reshape(slots)
-    picked_residual = take_rows(residual, flat)
-    tangent = (take_rows(cotangent, flat).astype(F32) * weight).astype(BF16)
+    picked_residual = take_rows(residual_now, flat)
+    tangent = (take_rows(cotangent_now, flat).astype(F32) * weight).astype(BF16)
     all_tangents = lax.all_gather(tangent.reshape(experts, SLOTS, width), "ep", axis=0)
     own_tangents = lax.dynamic_index_in_dim(all_tangents, lax.axis_index("ep"), 1, False)
-    owned_tangent = lax.all_gather(own_tangents.reshape(-1, width), "sp", axis=0)
+    own_tangents = own_tangents.reshape(-1, width)
+    qkv, picked_residual = lax.optimization_barrier((qkv, picked_residual))
+    owned_tangent = lax.all_gather(own_tangents, "sp", axis=0)
 
     query_rows = (flat // rows) * (3 * rows) + flat % rows
     picked_queries = take_rows(qkv.reshape(-1, HD), query_rows)
@@ -397,7 +498,6 @@
         block,
         "picked_attention",
     )
-
     def full_attention(first, count, queries_here):
         return attention(
             queries_here,
@@ -410,17 +510,36 @@
             "full_attention",
         )
 
+    to_rows = jnp.broadcast_to(
+        picked_hidden.reshape(experts, 1, SLOTS, width), (experts, side, SLOTS, width)
+    )
     owned = lax.all_to_all(
-        picked_hidden.reshape(experts, SLOTS, width), "ep", split_axis=0, concat_axis=0, tiled=True
-    ).reshape(-1, width)
+        to_rows.reshape(-1, SLOTS, width),
+        ("ep", "sp"),
+        split_axis=0,
+        concat_axis=0,
+        axis_index_groups=[
+            [e * group + x * side + y for e in range(experts) for y in range(side)]
+            for x in range(side)
+        ],
+        tiled=True,
+    )
     half = group // 4
     owned, queries_now = lax.optimization_barrier((owned, qkv))
-    owned_rows = spread(owned)
+    copies = jnp.broadcast_to(owned[None], (side,) + owned.shape)
+    owned_rows = lax.all_to_all(
+        copies.reshape(side, -1, width),
+        "sp",
+        split_axis=0,
+        concat_axis=0,
+        axis_index_groups=x_groups,
+        tiled=True,
+    ).reshape(side, experts, side, SLOTS, width)
     hidden_first = full_attention(0, half, queries_now)
     gate, up, down = gate_proj[0], up_proj[0], down_proj[0]
     d_act = tangent_product(owned_tangent, down)
     owned_rows, d_act, hidden_first = lax.optimization_barrier((owned_rows, d_act, hidden_first))
-    act, out_part, *grad_parts = expert(y_me, owned_rows, d_act, gate, up, down, side)
+    act, out_part, *grad_parts = expert(y_me, owned_rows, d_act, gate, up, down)
 
     act, out_part, queries_now = lax.optimization_barrier((act, out_part, qkv))
     out_part = lax.all_to_all(
@@ -437,7 +556,7 @@
     out_part, grad_down, hidden_second = lax.optimization_barrier(
         (out_part, grad_down, hidden_second)
     )
-    out_part = jnp.sum(out_part.astype(F32).reshape(side, side, -1, width), axis=0).astype(BF16)
+    out_part = quarter_sum(out_part.reshape(side, side, -1, width))
     out_part = lax.all_to_all(
         out_part, "sp", split_axis=0, concat_axis=0, axis_index_groups=y_groups, tiled=True
     )

time: 227 us -> 218 us (0.960)
  blocking collectives: 20.5 us -> 31.1 us
  waiting for transfers between devices: 59.9 us -> 50.8 us
  local copies, waits for them, and re-layouts: 26.5 us -> 18.9 us
  other arithmetic: 5.7 us -> 3.05 us
    all_to_all x1, blocking collectives: 20.5 us -> 31.1 us  [on_device(): lax.all_to_all(to_rows.reshape(-1, SLOTS, width), ('ep', 'sp'), split_axi...]
    unnamed x44 -> x34, local copies, waits for them, and re-layouts: 15.7 us -> 8.51 us
    all_to_all x1, waiting for transfers between devices: 9.23 us -> 2.32 us  [on_device(): lax.all_to_all(copies.reshape(side, -1, width), 'sp', split_axis=0, conca...]
    all_gather x1, waiting for transfers between devices: 31.9 us -> 36.3 us  [on_device(): lax.all_gather(tangent.reshape(experts, SLOTS, width), 'ep', axis=0)]
    all_to_all x1, waiting for transfers between devices: 4.28 us -> 0.01 us  [on_device(): qkv = lax.all_to_all(packed, 'sp', split_axis=0, concat_axis=0, tiled=True)]
    all_to_all x1, starting transfers between devices: 7.86 us -> 11.5 us  [on_device(): back = lax.all_to_all(back, 'ep', split_axis=0, concat_axis=0, tiled=True)]
    reduce_sum x1 -> x0, other arithmetic: 2.89 us -> none  [on_device(): jnp.sum(out_part.astype(F32).reshape(side, side, -1, width), axis=0)]
    pallas_call x1 -> x2, Pallas kernels: 4.35 us -> 4.85 us  [the longest x1 3.82 us: pack(): pl.pallas_call(pack_kernel, in_specs=[hbm] * 3, out_specs=hbm, out_shape=...]
  transfers between devices with their start and end apart: 13 -> 13, of which waited for: 7 -> 5; matrix products, arithmetic and copies ran while one was open for 5% -> 5% of each run, Pallas kernels for 20% -> 20%
where the time goes in v2:
time: 218 us; the launch traced here: 217 us
  Pallas kernels  58.2 us (27%)
  waiting for transfers between devices  50.8 us (23%)
  starting transfers between devices  40.8 us (19%)
  blocking collectives  31.1 us (14%)
  local copies, waits for them, and re-layouts  18.9 us (9%)
  between operations  14.3 us (7%)
  other arithmetic  3.05 us (1%)
    pallas_call x3, Pallas kernels, attention(): pl.pallas_call(functools.partial(attention_kernel, rows), grid=(total //...  37.4 us
    all_gather x1, waiting for transfers between devices, on_device(): lax.all_gather(tangent.reshape(experts, SLOTS, width), 'ep', axis=0)  36.3 us
    all_to_all x1, blocking collectives, on_device(): lax.all_to_all(to_rows.reshape(-1, SLOTS, width), ('ep', 'sp'), split_axi...  31.1 us
    all_to_all x1, starting transfers between devices, on_device(): back = lax.all_to_all(back, 'ep', split_axis=0, concat_axis=0, tiled=True)  11.5 us
    all_to_all x1, waiting for transfers between devices, on_device(): back = lax.all_to_all(back, 'ep', split_axis=0, concat_axis=0, tiled=True)  9.6 us
    ppermute x6, starting transfers between devices, shift(): return lax.ppermute(block, 'sp', moves)  8.84 us
    unnamed x34, local copies, waits for them, and re-layouts  8.51 us
    pallas_call x1, Pallas kernels, expert(): pl.pallas_call(expert_kernel, in_specs=[pl.BlockSpec(memory_space=pltpu.S...  7.75 us
  transfers between devices with their start and end apart: 13, of which 5 were waited for; matrix products, arithmetic and copies ran while one was open for 5% of the time, Pallas kernels for 20%

profile of v2, /device:TPU:1, one launch (start us, length us, event | category | flops | bytes accessed | tf_op | source)
XLA Modules:
  0.0 217.0 jit_solution(80680170166396332)
XLA Ops:
  7.2 0.8 reshape_squeeze.3
  8.0 3.8 %pack_qkv.1 = bf16[16,768,128]{2,1,0:T(8,128)(2,1)} custom-call(bf16[256,2048]{1,0:T(8,128)(2,1)} %q_hbm.1, bf16[256,2048]{1,0:T(8,128)(2,1)} %k_hbm.1, bf16[256,2048]{1,0:T(8,128)(2,1)} %v_hbm.1), custom_call_target="tpu_custom_call" | custom-call | tf_op jit(solution)/shard_map/pack_qkv/pallas_call | solution.py:58
  11.9 1.3 gather_fusion.2
  13.2 0.1 bitcast_select_fusion
  13.3 0.8 fusion
  14.1 7.6 %all-to-all-start = ((bf16[16,768,128]{2,1,0:T(8,128)(2,1)}), bf16[16,768,128]{2,1,0:T(8,128)(2,1)S(1)}, u32[]{:S(2)}, u32[]{:S(2)}) async-start(bf16[16,768,128]{2,1,0:T(8,128)(2,1)} %pack_qkv.1), calls=%async_computation | async-start | bytes 6291456 | tf_op jit(solution)/shard_map/all_to_all | solution.py:476
  21.8 36.3 %all-gather.3.cloned.1.call-done = bf16[16,16,32,128]{3,2,1,0:T(8,128)(2,1)} async-done(((bf16[1,16,32,128]{3,2,1,0:T(8,128)(2,1)}), bf16[16,16,32,128]{3,2,1,0:T(8,128)(2,1)}) %all-gather.3.cloned.1.call-update) | async-done | bytes 2097168 | tf_op jit(solution)/shard_map/all_gather | solution.py:482
  58.1 1.6 constant_dynamic-slice_fusion
  59.6 2.4 %gather_fusion = bf16[512,128]{1,0:T(8,128)(2,1)S(1)} fusion(bf16[4096,128]{1,0:T(8,128)(2,1)} %res_ref.3, s32[1024]{0:T(1024)S(1)} %get-tuple-element.68), kind=kCustom, calls=%fused_computation | custom fusion | bytes 264192 | tf_op jit(solution)/shard_map/gather | solution.py:434
  62.1 1.3 gather_fusion.1
  63.4 4.5 %picked_attention.1 = bf16[512,128]{1,0:T(8,128)(2,1)S(1)} custom-call(bf16[512,128]{1,0:T(8,128)(2,1)S(1)} %gather_fusion.1, bf16[512,128]{1,0:T(8,128)(2,1)S(1)} %gather_fusion, bf16[16,768,128]{2,1,0:T(8,128)(2,1)S(1)} %all-to-all-done.qkv_ref.q_ref), custom_call_target="tpu_custom_call" | custom-call | flops 2147483648 | bytes 3670016 | tf_op jit(solution)/shard_map/picked_attention/pallas_call | solution.py:140
  67.9 0.1 broadcast_in_dim.36
  68.0 31.1 %all_to_all.30 = bf16[64,32,128]{2,1,0:T(8,128)(2,1)S(1)} all-to-all(bf16[64,32,128]{2,1,0:T(8,128)(2,1)S(1)} %bitcast.30), channel_id=1, replica_groups={{0,1,2,3,16,17,18,19,32,33,34,35,48,49,50,51,64,65,66,67,80,81,82,83,96..., dimensions={0} | all-to-all | bytes 1048576 | tf_op jit(solution)/shard_map/all_to_all | solution.py:516
  99.1 1.6 broadcast_in_dim.38
  100.7 5.5 %all-to-all-start.2 = ((bf16[4,2048,128]{2,1,0:T(8,128)(2,1)}), bf16[4,2048,128]{2,1,0:T(8,128)(2,1)}, u32[]{:S(2)}, u32[]{:S(2)}) async-start(bf16[4,2048,128]{2,1,0:T(8,128)(2,1)} %broadcast_in_dim.38), calls=%async_computation.2 | async-start | bytes 4194304 | tf_op jit(solution)/shard_map/all_to_all | solution.py:530
  106.2 1.2 copy-done.7
  107.4 16.4 %full_attention.2 = bf16[2048,128]{1,0:T(8,128)(2,1)S(1)} custom-call(bf16[16,768,128]{2,1,0:T(8,128)(2,1)S(1)} %all-to-all-done.qkv_ref.q_ref, bf16[4096,128]{1,0:T(8,128)(2,1)S(1)} %copy-done.7, bf16[16,768,128]{2,1,0:T(8,128)(2,1)S(1)} %all-to-all-done.qkv_ref.q_ref), custom_call_target="tpu_custom_call" | custom-call | flops 8589934592 | bytes 5242880 | tf_op jit(solution)/shard_map/full_attention/pallas_call | solution.py:140
  123.9 0.8 copy-done.11
  124.6 1.6 copy-done
  126.2 1.2 copy-done.6
  127.5 0.7 tangent_product.1.d_act_hbm
  128.2 0.8 copy-done.10
  129.0 2.3 %all-to-all-done.2 = bf16[4,2048,128]{2,1,0:T(8,128)(2,1)} async-done(((bf16[4,2048,128]{2,1,0:T(8,128)(2,1)}), bf16[4,2048,128]{2,1,0:T(8,128)(2,1)}, u32[]{:S(2)}, u32[]{:S(2)}) %all-to-all-start.2) | async-done | bytes 2097184 | tf_op jit(solution)/shard_map/all_to_all | solution.py:530
  131.3 7.7 %expert.1 = (bf16[512,256]{1,0:T(8,128)(2,1)}, bf16[16,512,128]{2,1,0:T(8,128)(2,1)}, bf16[4,512,128]{2,1,0:T(8,128)(2,1)}, bf16[4,512,128]{2,1,0:T(8,128)(2,1)}...) custom-call(s32[1]{0:T(128)} %bitcast.2.me_ref, bf16[4,16,4,32,128]{4,3,2,1,0:T(8,128)(2,1)} %bitcast.7.x_hbm, ...), custom_call_target="tpu_custom_call" | custom-call | flops 2684354560 | bytes 7077888 | tf_op jit(solution)/shard_map/expert/pallas_call | solution.py:279
  139.1 3.8 %all-to-all-start.3 = ((bf16[4,2048,128]{2,1,0:T(8,128)(2,1)}), bf16[4,2048,128]{2,1,0:T(8,128)(2,1)S(1)}, u32[]{:S(2)}, u32[]{:S(2)}) async-start(bf16[4,2048,128]{2,1,0:T(8,128)(2,1)} %bitcast.31), calls=%async_computation.3 | async-start | bytes 4194304 | tf_op jit(solution)/shard_map/all_to_all | solution.py:545
  142.8 1.1 collective-permute-start
  143.9 2.6 %collective-permute-start.1 = (bf16[4,512,128]{2,1,0:T(8,128)(2,1)}, bf16[4,512,128]{2,1,0:T(8,128)(2,1)}, u32[]{:S(2)}, u32[]{:S(2)}) collective-permute-start(bf16[4,512,128]{2,1,0:T(8,128)(2,1)} %get-tuple-element.54), channel_id=1, source_target_pairs={{0,2},{1,3},{2,0},{3,1},{4,6},{5,7},{6,4},{7,5},{8,10},{9,11},{10,... | collective-permute-start | bytes 1572872 | tf_op jit(solution)/shard_map/ppermute | solution.py:444
  146.5 0.2 collective-permute-start.2
  146.7 2.0 copy-done.3
  148.7 16.5 %full_attention.3 = bf16[2048,128]{1,0:T(8,128)(2,1)S(1)} custom-call(bf16[16,768,128]{2,1,0:T(8,128)(2,1)S(1)} %copy-done.3, bf16[4096,128]{1,0:T(8,128)(2,1)S(1)} %copy-done.8, bf16[16,768,128]{2,1,0:T(8,128)(2,1)S(1)} %copy-done.3), custom_call_target="tpu_custom_call" | custom-call | flops 8589934592 | bytes 5242880 | tf_op jit(solution)/shard_map/full_attention/pallas_call | solution.py:140
  165.2 0.8 copy-done.13
  166.0 1.7 down_grad.1
  167.7 1.0 quarter_sum.1
  168.8 3.5 %all-to-all-start.4 = ((bf16[4,512,128]{2,1,0:T(8,128)(2,1)}), bf16[4,512,128]{2,1,0:T(8,128)(2,1)S(1)}, u32[]{:S(2)}, u32[]{:S(2)}) async-start(bf16[4,512,128]{2,1,0:T(8,128)(2,1)} %quarter_sum.1), calls=%async_computation.4 | async-start | bytes 1048576 | tf_op jit(solution)/shard_map/all_to_all | solution.py:560
  172.3 1.0 squeeze.21
  173.3 1.7 half_sum.1
  174.9 1.4 collective-permute-start.3
  176.3 2.4 %collective-permute-start.4 = (bf16[512,128]{1,0:T(8,128)(2,1)S(1)}, bf16[512,128]{1,0:T(8,128)(2,1)S(1)}, u32[]{:S(2)}, u32[]{:S(2)}) collective-permute-start(bf16[512,128]{1,0:T(8,128)(2,1)S(1)} %get-tuple-element.58), channel_id=1, source_target_pairs={{0,8},{1,9},{2,10},{3,11},{4,12},{5,13},{6,14},{7,15},{8,0},{9,1},... | collective-permute-start | bytes 393224 | tf_op jit(solution)/shard_map/ppermute | solution.py:444
  178.8 1.2 collective-permute-start.5
  179.9 0.1 iota_compare_fusion
  180.0 0.3 lt.59
  180.3 2.5 %collective-permute-done.4.refs_2_ = bf16[512,128]{1,0:T(8,128)(2,1)S(1)} collective-permute-done((bf16[512,128]{1,0:T(8,128)(2,1)S(1)}, bf16[512,128]{1,0:T(8,128)(2,1)S(1)}, u32[]{:S(2)}, u32[]{:S(2)}) %collective-permute-start.4) | collective-permute-done | bytes 131104 | tf_op jit(solution)/shard_map/ppermute | solution.py:444
  182.9 0.8 last_sum.1
  183.7 11.5 %all-to-all-start.5 = ((bf16[16,32,256]{2,1,0:T(8,128)(2,1)}), bf16[16,32,256]{2,1,0:T(8,128)(2,1)S(1)}, u32[]{:S(2)}, u32[]{:S(2)}) async-start(bf16[16,32,256]{2,1,0:T(8,128)(2,1)} %bitcast.17), calls=%async_computation.5 | async-start | bytes 524288 | tf_op jit(solution)/shard_map/all_to_all | solution.py:566
  195.2 1.0 broadcast_select_fusion.weight_ref
  196.2 1.1 pad_maximum_fusion.hid_ref
  197.3 9.6 %all-to-all-done.5 = bf16[16,32,256]{2,1,0:T(8,128)(2,1)S(1)} async-done(((bf16[16,32,256]{2,1,0:T(8,128)(2,1)}), bf16[16,32,256]{2,1,0:T(8,128)(2,1)S(1)}, u32[]{:S(2)}, u32[]{:S(2)}) %all-to-all-start.5) | async-done | bytes 262176 | tf_op jit(solution)/shard_map/all_to_all | solution.py:566
  207.0 3.2 %combine.1 = (bf16[4096,128]{1,0:T(8,128)(2,1)}, bf16[4096,128]{1,0:T(8,128)(2,1)}) custom-call(s32[1,512]{1,0:T(1,128)S(1)} %bitcast.28, f32[512,1]{1,0:T(8,128)S(1)} %broadcast_select_fusion.weight_ref, bf16[512,256]{1,0:T(8,128)(2,1)S(1)} %bitcast.26, bf16[4096,128]{1,0:T(8,128)(2,1)S(1)} %pad_maximum_fusion.hid_ref, bf16[4096,128]{1,0:T(8,128)(2,1)S(1)} %copy-done.5), custom_call_target="tpu_custom_call" | custom-call | tf_op jit(solution)/shard_map/combine/pallas_call | solution.py:416
  (42 shorter events, 0.3 us)
Async XLA Ops:
  7.2 50.9 %all-gather.3.cloned.1.call-start = ((), (), s32[]{:S(2)}) async-start(), calls=%async_computation.6 | async-start | bytes 2228224 | tf_op jit(solution)/shard_map/all_gather | solution.py:482
  8.0 3.9 %copy-start.4 = (bf16[4096,128]{1,0:T(8,128)(2,1)S(1)}, bf16[4096,128]{1,0:T(8,128)(2,1)}, u32[]{:S(2)}) copy-start(bf16[4096,128]{1,0:T(8,128)(2,1)} %cot_ref.1) | copy-start | bytes 3145732
  8.0 5.2 %copy-start.15 = (f32[1,16,32]{2,1,0:T(8,128)S(1)}, f32[1,16,32]{2,1,0:T(8,128)}, u32[]{:S(2)}) copy-start(f32[1,16,32]{2,1,0:T(8,128)} %param.21) | copy-start | bytes 6148
  8.0 5.2 %copy-start.16 = (s32[1,16]{1,0:T(1,128)S(1)}, s32[1,16]{1,0:T(1,128)}, u32[]{:S(2)}) copy-start(s32[1,16]{1,0:T(1,128)} %param.20) | copy-start | bytes 196
  14.1 48.0 %all-to-all-start = ((bf16[16,768,128]{2,1,0:T(8,128)(2,1)}), bf16[16,768,128]{2,1,0:T(8,128)(2,1)S(1)}, u32[]{:S(2)}, u32[]{:S(2)}) async-start(bf16[16,768,128]{2,1,0:T(8,128)(2,1)} %pack_qkv.1), calls=%async_computation | async-start | bytes 6291456 | tf_op jit(solution)/shard_map/all_to_all | solution.py:476
  21.7 102.9 %all-gather.5.cloned.1.call-start = ((), (), s32[]{:S(2)}) async-start(), calls=%async_computation.7 | async-start | bytes 2228224 | tf_op jit(solution)/shard_map/all_gather | solution.py:486
  62.1 44.1 %copy-start.2 = (bf16[16,768,128]{2,1,0:T(8,128)(2,1)}, bf16[16,768,128]{2,1,0:T(8,128)(2,1)S(1)}, u32[]{:S(2)}) copy-start(bf16[16,768,128]{2,1,0:T(8,128)(2,1)S(1)} %all-to-all-done.qkv_ref.q_ref) | copy-start | bytes 9437188
  100.7 30.7 %all-to-all-start.2 = ((bf16[4,2048,128]{2,1,0:T(8,128)(2,1)}), bf16[4,2048,128]{2,1,0:T(8,128)(2,1)}, u32[]{:S(2)}, u32[]{:S(2)}) async-start(bf16[4,2048,128]{2,1,0:T(8,128)(2,1)} %broadcast_in_dim.38), calls=%async_computation.2 | async-start | bytes 4194304 | tf_op jit(solution)/shard_map/all_to_all | solution.py:530
  106.2 1.2 copy-start.7
  123.8 0.8 copy-start.11
  124.6 1.6 copy-start
  126.2 1.2 copy-start.6
  128.2 0.8 copy-start.10
  139.1 7.6 %copy-start.8 = (bf16[4096,128]{1,0:T(8,128)(2,1)S(1)}, bf16[4096,128]{1,0:T(8,128)(2,1)}, u32[]{:S(2)}) copy-start(bf16[4096,128]{1,0:T(8,128)(2,1)} %res_ref.3) | copy-start | bytes 3145732
  139.1 28.7 %all-to-all-start.3 = ((bf16[4,2048,128]{2,1,0:T(8,128)(2,1)}), bf16[4,2048,128]{2,1,0:T(8,128)(2,1)S(1)}, u32[]{:S(2)}, u32[]{:S(2)}) async-start(bf16[4,2048,128]{2,1,0:T(8,128)(2,1)} %bitcast.31), calls=%async_computation.3 | async-start | bytes 4194304 | tf_op jit(solution)/shard_map/all_to_all | solution.py:545
  142.8 30.4 %collective-permute-start = (bf16[4,512,128]{2,1,0:T(8,128)(2,1)}, bf16[4,512,128]{2,1,0:T(8,128)(2,1)}, u32[]{:S(2)}, u32[]{:S(2)}) collective-permute-start(bf16[4,512,128]{2,1,0:T(8,128)(2,1)} %get-tuple-element.53), channel_id=1, source_target_pairs={{0,1},{1,2},{2,3},{3,0},{4,5},{5,6},{6,7},{7,4},{8,9},{9,10},{10,1... | collective-permute-start | bytes 1572872 | tf_op jit(solution)/shard_map/ppermute | solution.py:444
  143.9 29.3 %collective-permute-start.1 = (bf16[4,512,128]{2,1,0:T(8,128)(2,1)}, bf16[4,512,128]{2,1,0:T(8,128)(2,1)}, u32[]{:S(2)}, u32[]{:S(2)}) collective-permute-start(bf16[4,512,128]{2,1,0:T(8,128)(2,1)} %get-tuple-element.54), channel_id=1, source_target_pairs={{0,2},{1,3},{2,0},{3,1},{4,6},{5,7},{6,4},{7,5},{8,10},{9,11},{10,... | collective-permute-start | bytes 1572872 | tf_op jit(solution)/shard_map/ppermute | solution.py:444
  146.5 19.5 %copy-start.1 = (bf16[16,512,128]{2,1,0:T(8,128)(2,1)S(1)}, bf16[16,512,128]{2,1,0:T(8,128)(2,1)}, u32[]{:S(2)}) copy-start(bf16[16,512,128]{2,1,0:T(8,128)(2,1)} %all-gather.5.cloned.1.call-done.tan_ref) | copy-start | bytes 6291460
  146.5 26.7 %collective-permute-start.2 = (bf16[4,512,128]{2,1,0:T(8,128)(2,1)}, bf16[4,512,128]{2,1,0:T(8,128)(2,1)}, u32[]{:S(2)}, u32[]{:S(2)}) collective-permute-start(bf16[4,512,128]{2,1,0:T(8,128)(2,1)} %get-tuple-element.55), channel_id=1, source_target_pairs={{0,3},{1,0},{2,1},{3,2},{4,7},{5,4},{6,5},{7,6},{8,11},{9,8},{10,9... | collective-permute-start | bytes 1572872 | tf_op jit(solution)/shard_map/ppermute | solution.py:444
  146.7 2.0 copy-start.3
  148.7 17.3 %copy-start.14 = (bf16[512,256]{1,0:T(8,128)(2,1)S(1)}, bf16[512,256]{1,0:T(8,128)(2,1)}, u32[]{:S(2)}) copy-start(bf16[512,256]{1,0:T(8,128)(2,1)} %get-tuple-element.49.act_ref) | copy-start | bytes 786436
  165.2 0.9 copy-start.13
  167.7 5.5 %copy-start.9 = (bf16[4,512,128]{2,1,0:T(8,128)(2,1)S(1)}, bf16[4,512,128]{2,1,0:T(8,128)(2,1)}, u32[]{:S(2)}) copy-start(bf16[4,512,128]{2,1,0:T(8,128)(2,1)} %get-tuple-element.52.refs_0_) | copy-start | bytes 1572868
  168.8 14.1 %all-to-all-start.4 = ((bf16[4,512,128]{2,1,0:T(8,128)(2,1)}), bf16[4,512,128]{2,1,0:T(8,128)(2,1)S(1)}, u32[]{:S(2)}, u32[]{:S(2)}) async-start(bf16[4,512,128]{2,1,0:T(8,128)(2,1)} %quarter_sum.1), calls=%async_computation.4 | async-start | bytes 1048576 | tf_op jit(solution)/shard_map/all_to_all | solution.py:560
  173.2 23.0 %copy-start.12 = (bf16[2048,128]{1,0:T(8,128)(2,1)S(1)}, bf16[2048,128]{1,0:T(8,128)(2,1)}, u32[]{:S(2)}) copy-start(bf16[2048,128]{1,0:T(8,128)(2,1)} %copy-done.11) | copy-start | bytes 1572868
  174.9 5.4 %collective-permute-start.3 = (bf16[512,128]{1,0:T(8,128)(2,1)S(1)}, bf16[512,128]{1,0:T(8,128)(2,1)S(1)}, u32[]{:S(2)}, u32[]{:S(2)}) collective-permute-start(bf16[512,128]{1,0:T(8,128)(2,1)S(1)} %get-tuple-element.57), channel_id=1, source_target_pairs={{0,4},{1,5},{2,6},{3,7},{4,8},{5,9},{6,10},{7,11},{8,12},{9,13},{1... | collective-permute-start | bytes 393224 | tf_op jit(solution)/shard_map/ppermute | solution.py:444
  176.3 6.5 %collective-permute-start.4 = (bf16[512,128]{1,0:T(8,128)(2,1)S(1)}, bf16[512,128]{1,0:T(8,128)(2,1)S(1)}, u32[]{:S(2)}, u32[]{:S(2)}) collective-permute-start(bf16[512,128]{1,0:T(8,128)(2,1)S(1)} %get-tuple-element.58), channel_id=1, source_target_pairs={{0,8},{1,9},{2,10},{3,11},{4,12},{5,13},{6,14},{7,15},{8,0},{9,1},... | collective-permute-start | bytes 393224 | tf_op jit(solution)/shard_map/ppermute | solution.py:444
  178.8 4.1 %collective-permute-start.5 = (bf16[512,128]{1,0:T(8,128)(2,1)S(1)}, bf16[512,128]{1,0:T(8,128)(2,1)S(1)}, u32[]{:S(2)}, u32[]{:S(2)}) collective-permute-start(bf16[512,128]{1,0:T(8,128)(2,1)S(1)} %get-tuple-element.59), channel_id=1, source_target_pairs={{0,12},{1,13},{2,14},{3,15},{4,0},{5,1},{6,2},{7,3},{8,4},{9,5},{1... | collective-permute-start | bytes 393224 | tf_op jit(solution)/shard_map/ppermute | solution.py:444
  182.9 24.1 %copy-start.5 = (bf16[4096,128]{1,0:T(8,128)(2,1)S(1)}, bf16[4096,128]{1,0:T(8,128)(2,1)}, u32[]{:S(2)}) copy-start(bf16[4096,128]{1,0:T(8,128)(2,1)} %cot_ref.1) | copy-start | bytes 3145732
  183.7 23.2 %all-to-all-start.5 = ((bf16[16,32,256]{2,1,0:T(8,128)(2,1)}), bf16[16,32,256]{2,1,0:T(8,128)(2,1)S(1)}, u32[]{:S(2)}, u32[]{:S(2)}) async-start(bf16[16,32,256]{2,1,0:T(8,128)(2,1)} %bitcast.17), calls=%async_computation.5 | async-start | bytes 524288 | tf_op jit(solution)/shard_map/all_to_all | solution.py:566
Sparse Core Ops, SparseCore 0:
  14.2 43.7 all-gather.2
  61.1 48.8 all-gather.4

commit v3 on v2

--- a/solution.py
+++ b/solution.py
@@ -23,29 +23,40 @@
     return pltpu.CompilerParams(vmem_limit_bytes=limit)
 
 
-def pack_kernel(q_hbm, k_hbm, v_hbm, out_hbm, stage_ref, in_sems, out_sems):
+def in_pieces(src, dst, sems, first, pieces=4):
+    rows = src.shape[0] // pieces
+    return [
+        pltpu.make_async_copy(
+            src.at[pl.ds(i * rows, rows)], dst.at[pl.ds(i * rows, rows)], sems.at[first + i]
+        )
+        for i in range(pieces)
+    ]
+
+
+def pack_kernel(q_hbm, k_hbm, v_hbm, out_hbm, q_ref, k_ref, v_ref, in_sems, out_sems):
     rows, width = q_hbm.shape
     heads = width // HD
-    sources = (q_hbm, k_hbm, v_hbm)
-    loads = []
-    for h in range(heads):
-        for i, ref in enumerate(sources):
-            loads.append(
+    refs = (q_ref, k_ref, v_ref)
+    loads = [
+        in_pieces(src, dst, in_sems, 4 * i)
+        for i, (src, dst) in enumerate(zip((q_hbm, k_hbm, v_hbm), refs))
+    ]
+    for pieces in loads:
+        for copy in pieces:
+            copy.start()
+    stores = []
+    for i, ref in enumerate(refs):
+        for copy in loads[i]:
+            copy.wait()
+        for h in range(heads):
+            stores.append(
                 pltpu.make_async_copy(
                     ref.at[:, pl.ds(h * HD, HD)],
-                    stage_ref.at[h, pl.ds(i * rows, rows), :],
-                    in_sems.at[3 * h + i],
+                    out_hbm.at[h, pl.ds(i * rows, rows), :],
+                    out_sems.at[heads * i + h],
                 )
             )
-    for copy in loads:
-        copy.start()
-    stores = [
-        pltpu.make_async_copy(stage_ref.at[h], out_hbm.at[h], out_sems.at[h]) for h in range(heads)
-    ]
-    for h in range(heads):
-        for copy in loads[3 * h : 3 * h + 3]:
-            copy.wait()
-        stores[h].start()
+            stores[-1].start()
     for copy in stores:
         copy.wait()
 
@@ -53,18 +64,14 @@
 def pack(queries, keys, values):
     rows, width = queries.shape
     heads = width // HD
-    shape = (heads, 3 * rows, HD)
     hbm = pl.BlockSpec(memory_space=pltpu.HBM)
     return pl.pallas_call(
         pack_kernel,
         in_specs=[hbm] * 3,
         out_specs=hbm,
-        out_shape=jax.ShapeDtypeStruct(shape, BF16),
-        scratch_shapes=[
-            pltpu.VMEM(shape, BF16),
-            pltpu.SemaphoreType.DMA((3 * heads,)),
-            pltpu.SemaphoreType.DMA((heads,)),
-        ],
+        out_shape=jax.ShapeDtypeStruct((heads, 3 * rows, HD), BF16),
+        scratch_shapes=[pltpu.VMEM(queries.shape, BF16)] * 3
+        + [pltpu.SemaphoreType.DMA((12,)), pltpu.SemaphoreType.DMA((3 * heads,))],
         compiler_params=params(BIG_VMEM),
         name="pack_qkv",
     )(queries, keys, values)
@@ -182,16 +189,6 @@
         ),
         name="tangent_product",
     )(tangent, down)
-
-
-def in_pieces(src, dst, sems, first, pieces=4):
-    rows = src.shape[0] // pieces
-    return [
-        pltpu.make_async_copy(
-            src.at[pl.ds(i * rows, rows)], dst.at[pl.ds(i * rows, rows)], sems.at[first + i]
-        )
-        for i in range(pieces)
-    ]
 
 
 def expert_kernel(
@@ -538,7 +535,9 @@
     hidden_first = full_attention(0, half, queries_now)
     gate, up, down = gate_proj[0], up_proj[0], down_proj[0]
     d_act = tangent_product(owned_tangent, down)
-    owned_rows, d_act, hidden_first = lax.optimization_barrier((owned_rows, d_act, hidden_first))
+    owned_rows, d_act, hidden_first, weight = lax.optimization_barrier(
+        (owned_rows, d_act, hidden_first, weight)
+    )
     act, out_part, *grad_parts = expert(y_me, owned_rows, d_act, gate, up, down)
 
     act, out_part, queries_now = lax.optimization_barrier((act, out_part, qkv))

time: 218 us -> 217 us (level)
    all_to_all x1, waiting for transfers between devices: 2.32 us -> 0.01 us  [on_device(): lax.all_to_all(copies.reshape(side, -1, width), 'sp', split_axis=0, conca...]
  transfers between devices with their start and end apart: 13 -> 13, of which waited for: 5 -> 4; matrix products, arithmetic and copies ran while one was open for 5% -> 5% of each run, Pallas kernels for 20% -> 20%
where the time goes in v3:
time: 217 us; the launch traced here: 216 us
  Pallas kernels  57.8 us (27%)
  waiting for transfers between devices  49.8 us (23%)
  starting transfers between devices  41 us (19%)
  blocking collectives  31.1 us (14%)
  local copies, waits for them, and re-layouts  18.8 us (9%)
  between operations  14.3 us (7%)
  other arithmetic  3.05 us (1%)
    pallas_call x3, Pallas kernels, attention(): pl.pallas_call(functools.partial(attention_kernel, rows), grid=(total //...  37.4 us
    all_gather x1, waiting for transfers between devices, on_device(): lax.all_gather(tangent.reshape(experts, SLOTS, width), 'ep', axis=0)  36.3 us
    all_to_all x1, blocking collectives, on_device(): lax.all_to_all(to_rows.reshape(-1, SLOTS, width), ('ep', 'sp'), split_axi...  31.1 us
    all_to_all x1, waiting for transfers between devices, on_device(): back = lax.all_to_all(back, 'ep', split_axis=0, concat_axis=0, tiled=True)  10.6 us
    all_to_all x1, starting transfers between devices, on_device(): back = lax.all_to_all(back, 'ep', split_axis=0, concat_axis=0, tiled=True)  10.6 us
    ppermute x6, starting transfers between devices, shift(): return lax.ppermute(block, 'sp', moves)  8.92 us
    unnamed x34, local copies, waits for them, and re-layouts  8.39 us
    pallas_call x1, Pallas kernels, expert(): pl.pallas_call(expert_kernel, in_specs=[pl.BlockSpec(memory_space=pltpu.S...  7.75 us
  transfers between devices with their start and end apart: 13, of which 4 were waited for; matrix products, arithmetic and copies ran while one was open for 5% of the time, Pallas kernels for 20%

profile of v3, /device:TPU:1, one launch (start us, length us, event | category | flops | bytes accessed | tf_op | source)
XLA Modules:
  0.0 215.8 jit_solution(15746307394988268162)
XLA Ops:
  7.2 0.8 reshape_squeeze.3
  8.0 3.5 %pack_qkv.1 = bf16[16,768,128]{2,1,0:T(8,128)(2,1)} custom-call(bf16[256,2048]{1,0:T(8,128)(2,1)} %q_hbm.1, bf16[256,2048]{1,0:T(8,128)(2,1)} %k_hbm.1, bf16[256,2048]{1,0:T(8,128)(2,1)} %v_hbm.1), custom_call_target="tpu_custom_call" | custom-call | tf_op jit(solution)/shard_map/pack_qkv/pallas_call | solution.py:68
  11.5 0.1 bitcast_select_fusion
  11.6 1.3 gather_fusion.2
  12.9 0.8 fusion
  13.7 7.6 %all-to-all-start = ((bf16[16,768,128]{2,1,0:T(8,128)(2,1)}), bf16[16,768,128]{2,1,0:T(8,128)(2,1)S(1)}, u32[]{:S(2)}, u32[]{:S(2)}) async-start(bf16[16,768,128]{2,1,0:T(8,128)(2,1)} %pack_qkv.1), calls=%async_computation | async-start | bytes 6291456 | tf_op jit(solution)/shard_map/all_to_all | solution.py:473
  21.4 36.3 %all-gather.3.cloned.1.call-done = bf16[16,16,32,128]{3,2,1,0:T(8,128)(2,1)} async-done(((bf16[1,16,32,128]{3,2,1,0:T(8,128)(2,1)}), bf16[16,16,32,128]{3,2,1,0:T(8,128)(2,1)}) %all-gather.3.cloned.1.call-update) | async-done | bytes 2097168 | tf_op jit(solution)/shard_map/all_gather | solution.py:479
  57.7 1.6 constant_dynamic-slice_fusion
  59.3 2.4 %gather_fusion = bf16[512,128]{1,0:T(8,128)(2,1)S(1)} fusion(bf16[4096,128]{1,0:T(8,128)(2,1)} %res_ref.3, s32[1024]{0:T(1024)S(1)} %get-tuple-element.70), kind=kCustom, calls=%fused_computation | custom fusion | bytes 264192 | tf_op jit(solution)/shard_map/gather | solution.py:431
  61.7 1.3 gather_fusion.1
  63.1 4.5 %picked_attention.1 = bf16[512,128]{1,0:T(8,128)(2,1)S(1)} custom-call(bf16[512,128]{1,0:T(8,128)(2,1)S(1)} %gather_fusion.1, bf16[512,128]{1,0:T(8,128)(2,1)S(1)} %gather_fusion, bf16[16,768,128]{2,1,0:T(8,128)(2,1)S(1)} %all-to-all-done.qkv_ref.q_ref), custom_call_target="tpu_custom_call" | custom-call | flops 2147483648 | bytes 3670016 | tf_op jit(solution)/shard_map/picked_attention/pallas_call | solution.py:147
  67.5 0.1 broadcast_in_dim.35
  67.6 31.1 %all_to_all.30 = bf16[64,32,128]{2,1,0:T(8,128)(2,1)S(1)} all-to-all(bf16[64,32,128]{2,1,0:T(8,128)(2,1)S(1)} %bitcast.30), channel_id=1, replica_groups={{0,1,2,3,16,17,18,19,32,33,34,35,48,49,50,51,64,65,66,67,80,81,82,83,96..., dimensions={0} | all-to-all | bytes 1048576 | tf_op jit(solution)/shard_map/all_to_all | solution.py:513
  98.7 1.6 broadcast_in_dim.37
  100.3 5.5 %all-to-all-start.2 = ((bf16[4,2048,128]{2,1,0:T(8,128)(2,1)}), bf16[4,2048,128]{2,1,0:T(8,128)(2,1)}, u32[]{:S(2)}, u32[]{:S(2)}) async-start(bf16[4,2048,128]{2,1,0:T(8,128)(2,1)} %broadcast_in_dim.37), calls=%async_computation.2 | async-start | bytes 4194304 | tf_op jit(solution)/shard_map/all_to_all | solution.py:527
  105.8 1.0 squeeze.21
  106.8 0.1 iota_compare_fusion
  106.9 0.3 lt.59
  107.2 1.0 broadcast_select_fusion.weight_ref
  108.2 1.2 copy-done.7
  109.4 16.4 %full_attention.2 = bf16[2048,128]{1,0:T(8,128)(2,1)S(1)} custom-call(bf16[16,768,128]{2,1,0:T(8,128)(2,1)S(1)} %all-to-all-done.qkv_ref.q_ref, bf16[4096,128]{1,0:T(8,128)(2,1)S(1)} %copy-done.7, bf16[16,768,128]{2,1,0:T(8,128)(2,1)S(1)} %all-to-all-done.qkv_ref.q_ref), custom_call_target="tpu_custom_call" | custom-call | flops 8589934592 | bytes 5242880 | tf_op jit(solution)/shard_map/full_attention/pallas_call | solution.py:147
  125.8 0.8 copy-done.11
  126.6 1.6 copy-done
  128.2 1.2 copy-done.6
  129.5 0.7 tangent_product.1.d_act_hbm
  130.2 0.8 copy-done.10
  131.0 7.8 %expert.1 = (bf16[512,256]{1,0:T(8,128)(2,1)}, bf16[16,512,128]{2,1,0:T(8,128)(2,1)}, bf16[4,512,128]{2,1,0:T(8,128)(2,1)}, bf16[4,512,128]{2,1,0:T(8,128)(2,1)}...) custom-call(s32[1]{0:T(128)} %bitcast.11.me_ref, bf16[4,16,4,32,128]{4,3,2,1,0:T(8,128)(2,1)} %bitcast.5.x_hbm, ...), custom_call_target="tpu_custom_call" | custom-call | flops 2684354560 | bytes 7077888 | tf_op jit(solution)/shard_map/expert/pallas_call | solution.py:276
  138.8 4.8 %all-to-all-start.3 = ((bf16[4,2048,128]{2,1,0:T(8,128)(2,1)}), bf16[4,2048,128]{2,1,0:T(8,128)(2,1)S(1)}, u32[]{:S(2)}, u32[]{:S(2)}) async-start(bf16[4,2048,128]{2,1,0:T(8,128)(2,1)} %bitcast.31), calls=%async_computation.3 | async-start | bytes 4194304 | tf_op jit(solution)/shard_map/all_to_all | solution.py:544
  143.6 0.6 collective-permute-start
  144.2 2.4 %collective-permute-start.1 = (bf16[4,512,128]{2,1,0:T(8,128)(2,1)}, bf16[4,512,128]{2,1,0:T(8,128)(2,1)}, u32[]{:S(2)}, u32[]{:S(2)}) collective-permute-start(bf16[4,512,128]{2,1,0:T(8,128)(2,1)} %get-tuple-element.56), channel_id=1, source_target_pairs={{0,2},{1,3},{2,0},{3,1},{4,6},{5,7},{6,4},{7,5},{8,10},{9,11},{10,... | collective-permute-start | bytes 1572872 | tf_op jit(solution)/shard_map/ppermute | solution.py:441
  146.6 0.7 collective-permute-start.2
  147.4 1.9 copy-done.3
  149.3 16.4 %full_attention.3 = bf16[2048,128]{1,0:T(8,128)(2,1)S(1)} custom-call(bf16[16,768,128]{2,1,0:T(8,128)(2,1)S(1)} %copy-done.3, bf16[4096,128]{1,0:T(8,128)(2,1)S(1)} %copy-done.8, bf16[16,768,128]{2,1,0:T(8,128)(2,1)S(1)} %copy-done.3), custom_call_target="tpu_custom_call" | custom-call | flops 8589934592 | bytes 5242880 | tf_op jit(solution)/shard_map/full_attention/pallas_call | solution.py:147
  165.7 0.8 copy-done.13
  166.6 1.7 down_grad.1
  168.3 1.0 quarter_sum.1
  169.3 3.5 %all-to-all-start.4 = ((bf16[4,512,128]{2,1,0:T(8,128)(2,1)}), bf16[4,512,128]{2,1,0:T(8,128)(2,1)S(1)}, u32[]{:S(2)}, u32[]{:S(2)}) async-start(bf16[4,512,128]{2,1,0:T(8,128)(2,1)} %quarter_sum.1), calls=%async_computation.4 | async-start | bytes 1048576 | tf_op jit(solution)/shard_map/all_to_all | solution.py:559
  172.9 1.7 half_sum.1
  174.5 1.5 collective-permute-start.3
  176.1 2.4 %collective-permute-start.4 = (bf16[512,128]{1,0:T(8,128)(2,1)S(1)}, bf16[512,128]{1,0:T(8,128)(2,1)S(1)}, u32[]{:S(2)}, u32[]{:S(2)}) collective-permute-start(bf16[512,128]{1,0:T(8,128)(2,1)S(1)} %get-tuple-element.60), channel_id=1, source_target_pairs={{0,8},{1,9},{2,10},{3,11},{4,12},{5,13},{6,14},{7,15},{8,0},{9,1},... | collective-permute-start | bytes 393224 | tf_op jit(solution)/shard_map/ppermute | solution.py:441
  178.5 1.2 collective-permute-start.5
  179.7 2.9 %collective-permute-done.4.refs_2_ = bf16[512,128]{1,0:T(8,128)(2,1)S(1)} collective-permute-done((bf16[512,128]{1,0:T(8,128)(2,1)S(1)}, bf16[512,128]{1,0:T(8,128)(2,1)S(1)}, u32[]{:S(2)}, u32[]{:S(2)}) %collective-permute-start.4) | collective-permute-done | bytes 131104 | tf_op jit(solution)/shard_map/ppermute | solution.py:441
  182.5 0.1 collective-permute-done.5.refs_3_
  182.6 0.8 last_sum.1
  183.4 10.6 %all-to-all-start.5 = ((bf16[16,32,256]{2,1,0:T(8,128)(2,1)}), bf16[16,32,256]{2,1,0:T(8,128)(2,1)S(1)}, u32[]{:S(2)}, u32[]{:S(2)}) async-start(bf16[16,32,256]{2,1,0:T(8,128)(2,1)} %bitcast.17), calls=%async_computation.5 | async-start | bytes 524288 | tf_op jit(solution)/shard_map/all_to_all | solution.py:565
  194.0 1.1 pad_maximum_fusion.hid_ref
  195.1 10.6 %all-to-all-done.5 = bf16[16,32,256]{2,1,0:T(8,128)(2,1)S(1)} async-done(((bf16[16,32,256]{2,1,0:T(8,128)(2,1)}), bf16[16,32,256]{2,1,0:T(8,128)(2,1)S(1)}, u32[]{:S(2)}, u32[]{:S(2)}) %all-to-all-start.5) | async-done | bytes 262176 | tf_op jit(solution)/shard_map/all_to_all | solution.py:565
  205.7 3.2 %combine.1 = (bf16[4096,128]{1,0:T(8,128)(2,1)}, bf16[4096,128]{1,0:T(8,128)(2,1)}) custom-call(s32[1,512]{1,0:T(1,128)S(1)} %bitcast.28, f32[512,1]{1,0:T(8,128)S(1)} %broadcast_select_fusion.weight_ref, bf16[512,256]{1,0:T(8,128)(2,1)S(1)} %bitcast.26, bf16[4096,128]{1,0:T(8,128)(2,1)S(1)} %pad_maximum_fusion.hid_ref, bf16[4096,128]{1,0:T(8,128)(2,1)S(1)} %copy-done.5), custom_call_target="tpu_custom_call" | custom-call | tf_op jit(solution)/shard_map/combine/pallas_call | solution.py:413
  (42 shorter events, 0.2 us)
Async XLA Ops:
  7.2 50.5 %all-gather.3.cloned.1.call-start = ((), (), s32[]{:S(2)}) async-start(), calls=%async_computation.6 | async-start | bytes 2228224 | tf_op jit(solution)/shard_map/all_gather | solution.py:479
  8.0 3.5 %copy-start.15 = (f32[1,16,32]{2,1,0:T(8,128)S(1)}, f32[1,16,32]{2,1,0:T(8,128)}, u32[]{:S(2)}) copy-start(f32[1,16,32]{2,1,0:T(8,128)} %param.21) | copy-start | bytes 6148
  8.0 3.5 %copy-start.16 = (s32[1,16]{1,0:T(1,128)S(1)}, s32[1,16]{1,0:T(1,128)}, u32[]{:S(2)}) copy-start(s32[1,16]{1,0:T(1,128)} %param.20) | copy-start | bytes 196
  8.0 3.6 %copy-start.4 = (bf16[4096,128]{1,0:T(8,128)(2,1)S(1)}, bf16[4096,128]{1,0:T(8,128)(2,1)}, u32[]{:S(2)}) copy-start(bf16[4096,128]{1,0:T(8,128)(2,1)} %cot_ref.1) | copy-start | bytes 3145732
  13.7 48.0 %all-to-all-start = ((bf16[16,768,128]{2,1,0:T(8,128)(2,1)}), bf16[16,768,128]{2,1,0:T(8,128)(2,1)S(1)}, u32[]{:S(2)}, u32[]{:S(2)}) async-start(bf16[16,768,128]{2,1,0:T(8,128)(2,1)} %pack_qkv.1), calls=%async_computation | async-start | bytes 6291456 | tf_op jit(solution)/shard_map/all_to_all | solution.py:473
  21.4 105.3 %all-gather.5.cloned.1.call-start = ((), (), s32[]{:S(2)}) async-start(), calls=%async_computation.7 | async-start | bytes 2228224 | tf_op jit(solution)/shard_map/all_gather | solution.py:483
  61.7 46.4 %copy-start.2 = (bf16[16,768,128]{2,1,0:T(8,128)(2,1)}, bf16[16,768,128]{2,1,0:T(8,128)(2,1)S(1)}, u32[]{:S(2)}) copy-start(bf16[16,768,128]{2,1,0:T(8,128)(2,1)S(1)} %all-to-all-done.qkv_ref.q_ref) | copy-start | bytes 9437188
  100.3 30.7 %all-to-all-start.2 = ((bf16[4,2048,128]{2,1,0:T(8,128)(2,1)}), bf16[4,2048,128]{2,1,0:T(8,128)(2,1)}, u32[]{:S(2)}, u32[]{:S(2)}) async-start(bf16[4,2048,128]{2,1,0:T(8,128)(2,1)} %broadcast_in_dim.37), calls=%async_computation.2 | async-start | bytes 4194304 | tf_op jit(solution)/shard_map/all_to_all | solution.py:527
  108.2 1.2 copy-start.7
  125.8 0.8 copy-start.11
  126.6 1.6 copy-start
  128.2 1.2 copy-start.6
  130.2 0.8 copy-start.10
  138.8 8.6 %copy-start.8 = (bf16[4096,128]{1,0:T(8,128)(2,1)S(1)}, bf16[4096,128]{1,0:T(8,128)(2,1)}, u32[]{:S(2)}) copy-start(bf16[4096,128]{1,0:T(8,128)(2,1)} %res_ref.3) | copy-start | bytes 3145732
  138.8 29.5 %all-to-all-start.3 = ((bf16[4,2048,128]{2,1,0:T(8,128)(2,1)}), bf16[4,2048,128]{2,1,0:T(8,128)(2,1)S(1)}, u32[]{:S(2)}, u32[]{:S(2)}) async-start(bf16[4,2048,128]{2,1,0:T(8,128)(2,1)} %bitcast.31), calls=%async_computation.3 | async-start | bytes 4194304 | tf_op jit(solution)/shard_map/all_to_all | solution.py:544
  143.6 29.3 %collective-permute-start = (bf16[4,512,128]{2,1,0:T(8,128)(2,1)}, bf16[4,512,128]{2,1,0:T(8,128)(2,1)}, u32[]{:S(2)}, u32[]{:S(2)}) collective-permute-start(bf16[4,512,128]{2,1,0:T(8,128)(2,1)} %get-tuple-element.55), channel_id=1, source_target_pairs={{0,1},{1,2},{2,3},{3,0},{4,5},{5,6},{6,7},{7,4},{8,9},{9,10},{10,1... | collective-permute-start | bytes 1572872 | tf_op jit(solution)/shard_map/ppermute | solution.py:441
  144.2 28.6 %collective-permute-start.1 = (bf16[4,512,128]{2,1,0:T(8,128)(2,1)}, bf16[4,512,128]{2,1,0:T(8,128)(2,1)}, u32[]{:S(2)}, u32[]{:S(2)}) collective-permute-start(bf16[4,512,128]{2,1,0:T(8,128)(2,1)} %get-tuple-element.56), channel_id=1, source_target_pairs={{0,2},{1,3},{2,0},{3,1},{4,6},{5,7},{6,4},{7,5},{8,10},{9,11},{10,... | collective-permute-start | bytes 1572872 | tf_op jit(solution)/shard_map/ppermute | solution.py:441
  146.6 19.9 %copy-start.1 = (bf16[16,512,128]{2,1,0:T(8,128)(2,1)S(1)}, bf16[16,512,128]{2,1,0:T(8,128)(2,1)}, u32[]{:S(2)}) copy-start(bf16[16,512,128]{2,1,0:T(8,128)(2,1)} %all-gather.5.cloned.1.call-done.tan_ref) | copy-start | bytes 6291460
  146.6 26.2 %collective-permute-start.2 = (bf16[4,512,128]{2,1,0:T(8,128)(2,1)}, bf16[4,512,128]{2,1,0:T(8,128)(2,1)}, u32[]{:S(2)}, u32[]{:S(2)}) collective-permute-start(bf16[4,512,128]{2,1,0:T(8,128)(2,1)} %get-tuple-element.57), channel_id=1, source_target_pairs={{0,3},{1,0},{2,1},{3,2},{4,7},{5,4},{6,5},{7,6},{8,11},{9,8},{10,9... | collective-permute-start | bytes 1572872 | tf_op jit(solution)/shard_map/ppermute | solution.py:441
  147.4 1.9 copy-start.3
  149.3 17.3 %copy-start.14 = (bf16[512,256]{1,0:T(8,128)(2,1)S(1)}, bf16[512,256]{1,0:T(8,128)(2,1)}, u32[]{:S(2)}) copy-start(bf16[512,256]{1,0:T(8,128)(2,1)} %get-tuple-element.51.act_ref) | copy-start | bytes 786436
  165.7 0.9 copy-start.13
  168.3 4.6 %copy-start.9 = (bf16[4,512,128]{2,1,0:T(8,128)(2,1)S(1)}, bf16[4,512,128]{2,1,0:T(8,128)(2,1)}, u32[]{:S(2)}) copy-start(bf16[4,512,128]{2,1,0:T(8,128)(2,1)} %get-tuple-element.54.refs_0_) | copy-start | bytes 1572868
  169.3 13.3 %all-to-all-start.4 = ((bf16[4,512,128]{2,1,0:T(8,128)(2,1)}), bf16[4,512,128]{2,1,0:T(8,128)(2,1)S(1)}, u32[]{:S(2)}, u32[]{:S(2)}) async-start(bf16[4,512,128]{2,1,0:T(8,128)(2,1)} %quarter_sum.1), calls=%async_computation.4 | async-start | bytes 1048576 | tf_op jit(solution)/shard_map/all_to_all | solution.py:559
  172.8 21.2 %copy-start.12 = (bf16[2048,128]{1,0:T(8,128)(2,1)S(1)}, bf16[2048,128]{1,0:T(8,128)(2,1)}, u32[]{:S(2)}) copy-start(bf16[2048,128]{1,0:T(8,128)(2,1)} %copy-done.11) | copy-start | bytes 1572868
  174.5 31.2 %copy-start.5 = (bf16[4096,128]{1,0:T(8,128)(2,1)S(1)}, bf16[4096,128]{1,0:T(8,128)(2,1)}, u32[]{:S(2)}) copy-start(bf16[4096,128]{1,0:T(8,128)(2,1)} %cot_ref.1) | copy-start | bytes 3145732
  174.5 5.1 %collective-permute-start.3 = (bf16[512,128]{1,0:T(8,128)(2,1)S(1)}, bf16[512,128]{1,0:T(8,128)(2,1)S(1)}, u32[]{:S(2)}, u32[]{:S(2)}) collective-permute-start(bf16[512,128]{1,0:T(8,128)(2,1)S(1)} %get-tuple-element.59), channel_id=1, source_target_pairs={{0,4},{1,5},{2,6},{3,7},{4,8},{5,9},{6,10},{7,11},{8,12},{9,13},{1... | collective-permute-start | bytes 393224 | tf_op jit(solution)/shard_map/ppermute | solution.py:441
  176.1 6.4 %collective-permute-start.4 = (bf16[512,128]{1,0:T(8,128)(2,1)S(1)}, bf16[512,128]{1,0:T(8,128)(2,1)S(1)}, u32[]{:S(2)}, u32[]{:S(2)}) collective-permute-start(bf16[512,128]{1,0:T(8,128)(2,1)S(1)} %get-tuple-element.60), channel_id=1, source_target_pairs={{0,8},{1,9},{2,10},{3,11},{4,12},{5,13},{6,14},{7,15},{8,0},{9,1},... | collective-permute-start | bytes 393224 | tf_op jit(solution)/shard_map/ppermute | solution.py:441
  178.5 4.1 %collective-permute-start.5 = (bf16[512,128]{1,0:T(8,128)(2,1)S(1)}, bf16[512,128]{1,0:T(8,128)(2,1)S(1)}, u32[]{:S(2)}, u32[]{:S(2)}) collective-permute-start(bf16[512,128]{1,0:T(8,128)(2,1)S(1)} %get-tuple-element.61), channel_id=1, source_target_pairs={{0,12},{1,13},{2,14},{3,15},{4,0},{5,1},{6,2},{7,3},{8,4},{9,5},{1... | collective-permute-start | bytes 393224 | tf_op jit(solution)/shard_map/ppermute | solution.py:441
  183.4 22.3 %all-to-all-start.5 = ((bf16[16,32,256]{2,1,0:T(8,128)(2,1)}), bf16[16,32,256]{2,1,0:T(8,128)(2,1)S(1)}, u32[]{:S(2)}, u32[]{:S(2)}) async-start(bf16[16,32,256]{2,1,0:T(8,128)(2,1)} %bitcast.17), calls=%async_computation.5 | async-start | bytes 524288 | tf_op jit(solution)/shard_map/all_to_all | solution.py:565
Sparse Core Ops, SparseCore 0:
  13.9 43.7 all-gather.2
  60.7 48.8 all-gather.4
